TPU v7x, 128 devices: a whole 4x4x4 slice. The times are simulated.
128 devices in a mesh: node: 8 (over z, core), local: 16 (over x, y).
Axes of the slice: x: 4, y: 4, z: 4, core: 2. Of those that a mesh axis runs over, the one named last changes fastest.
Arguments:
- tokens: bfloat16 [2, 1024, 7168], P(None, ('node', 'local')), may hold values from -6 to 6
- routes: int32 [2, 1024, 8], P(None, ('node', 'local')), may hold values from 0 to 63, as said below
- route_weight: float32 [2, 1024, 8], P(None, ('node', 'local')), may hold values from 0.1 to 1
- gate_weight: bfloat16 [128, 7168, 512], P(('node', 'local')), may hold values from -0.0625 to 0.0625
- up_weight: bfloat16 [128, 7168, 512], P(('node', 'local')), may hold values from -0.0625 to 0.0625
- down_weight: bfloat16 [128, 512, 7168], P(('node', 'local')), may hold values from -0.1875 to 0.1875
Outputs:
- mixed: bfloat16 [2, 1024, 7168], P(None, ('node', 'local'))
Inputs may be any that keep to these rules, and one draw needn't show every extreme that they name: `routes`: node group g holds the experts e with e // 8 = g. Each token's choices lie in exactly 4 node groups, 2 in each, and no token chooses an expert twice. Among the 8 rows of one device in one micro-batch, no expert is chosen more than 2 times, and no node group is chosen by more than 8 tokens.
All inputs are finite; a program needn't handle non-finite values.
Results may differ from a plain program's by a relative error of at most 0.0058.
Values may be sent and summed in bfloat16 or wider, within the bound.
No kernel may reach another device: no remote copies, remote signals or barrier semaphores. Data moves between devices by JAX's collectives and lax.ppermute only.
A program may use at most 128 MiB of HBM per device.

v0:
```python
import functools

import jax
import jax.numpy as jnp
from jax import lax
from jax.experimental import pallas as pl
from jax.experimental.pallas import tpu as pltpu
from jax.sharding import PartitionSpec as P

AXES = ("node", "local")
ORDERS = (("x", "y", "z"), ("y", "z", "x"), ("z", "x", "y"))
RING = 4
META = 128
WIDE_PARAMS = pltpu.CompilerParams(vmem_limit_bytes=52 * 1024 * 1024)
PARAMS = pltpu.CompilerParams(vmem_limit_bytes=24 * 1024 * 1024)
BF16, F32 = jnp.bfloat16, jnp.float32


def device_index(place):
    return (place["z"] * 2 + place["c"]) * 16 + place["x"] * 4 + place["y"]


def all_places():
    return [
        {"z": z, "c": c, "x": x, "y": y}
        for z in range(4)
        for c in range(2)
        for x in range(4)
        for y in range(4)
    ]


def from_offset(value, axis, offset):
    size = 2 if axis == "c" else RING
    pairs = []
    for place in all_places():
        sign = -1 if place["c"] else 1
        target = dict(place)
        target[axis] = (place[axis] - sign * offset) % size
        pairs.append((device_index(place), device_index(target)))
    return lax.ppermute(value, AXES, pairs)


def column_split(width):
    tiles = width // 128
    sizes = [(tiles + 2 - k) // 3 * 128 for k in range(3)]
    starts = [sum(sizes[:k]) for k in range(3)]
    return starts, sizes


def cost(flops, nbytes):
    return pl.CostEstimate(flops=int(flops), bytes_accessed=int(nbytes), transcendentals=0)


def iota(shape, dim):
    return lax.broadcasted_iota(jnp.int32, shape, dim)


def prep_kernel(starts, sizes, tok_ref, info_ref, tok2_ref, info2_ref, *outs):
    half = tok_ref.shape[0]
    for part, (tok, info_in) in enumerate(((tok_ref, info_ref), (tok2_ref, info2_ref))):
        info = info_in[...]
        lane = iota(info.shape, 1)
        high = info.astype(BF16)
        low = (info - high.astype(F32)).astype(BF16)
        meta = jnp.where(lane < 16, high.astype(F32), low.astype(F32)).astype(BF16)
        at = slice(part * half, part * half + half)
        for k, (start, size) in enumerate(zip(starts, sizes, strict=True)):
            outs[k][at, :size] = tok[:, start : start + size]
            outs[k][at, size:] = meta
            if not part:
                outs[3 + k][:, :size] = tok[:, start : start + size]
                outs[3 + k][:, size:] = meta


def prepare(tokens, info, tokens2, info2, starts, sizes):
    rows = tokens.shape[0]
    return pl.pallas_call(
        functools.partial(prep_kernel, starts, sizes),
        out_shape=[jax.ShapeDtypeStruct((2 * rows, size + META), BF16) for size in sizes]
        + [jax.ShapeDtypeStruct((rows, size + META), BF16) for size in sizes],
        compiler_params=PARAMS,
        cost_estimate=cost(0, 10 * tokens.size),
        name="prep",
    )(tokens, info, tokens2, info2)


def slot_matrices(metas, experts):
    shape = metas[0].shape
    row, lane = iota(shape, 0), iota(shape, 1)
    near = (shape[0], shape[0])
    before = (iota(near, 0) // 8 == iota(near, 1) // 8) & (iota(near, 1) < iota(near, 0))
    before = jnp.where(before, 1.0, 0.0).astype(BF16)
    fits = row // 8 == lane % 16 // 2
    slot = (lane % 2).astype(F32)
    targets = [expert.astype(F32) for expert in experts]
    gained = []
    for meta in metas:
        meta = meta.astype(F32)
        gains = 4.0 + pltpu.roll(meta, META - 8, 1) + pltpu.roll(meta, META - 16, 1)
        value = jnp.zeros(shape, F32)
        for group in range(4):
            hit = (meta == targets[group]) & (lane < 8)
            gain = jnp.sum(jnp.where(hit, gains, 0.0), axis=1, keepdims=True)
            value = jnp.where(lane // 16 == group, gain, value)
        gained.append(value)
    chosen = [jnp.where(value > 2.0, 1.0, 0.0) for value in gained]
    ranks = jnp.dot(
        before,
        jnp.concatenate([picked.astype(BF16) for picked in chosen], axis=1),
        preferred_element_type=F32,
    )
    out = []
    for j, picked in enumerate(chosen):
        keep = (ranks[:, META * j : META * j + META] == slot) & fits & (picked > 0.5)
        out.append((jnp.where(keep, 1.0, 0.0), jnp.where(keep, gained[j] - 4.0, 0.0)))
    return out


def split_blocks(refs):
    chip, near, far, their_near, their_far = refs
    places = [(chip, 0), (near, 0), (near, 64), (far, 0)]
    places += [(chip, 64), (their_near, 0), (their_near, 64), (their_far, 0)]
    return [ref.at[pl.ds(at, 64)] for ref, at in places]


def pack_kernel(size, color, experts_ref, *refs):
    blocks, outs, gains = split_blocks(refs[:5]), refs[5:8], refs[8]
    experts = [experts_ref[color, group] for group in range(4)]
    matrices = slot_matrices([block[:, size:] for block in blocks], experts)
    slots = [matrix.T.astype(BF16)[:64] for matrix, _ in matrices]
    for j, block in enumerate(blocks):
        packed = jnp.dot(slots[j], block[:, :size], preferred_element_type=F32).astype(BF16)
        at = slice(16 * j, 16 * j + 16)
        outs[0][at, :] = packed[:16]
        outs[1][at, :] = packed[16:32]
        outs[1][128 + 16 * j : 128 + 16 * j + 16, :] = packed[32:48]
        outs[2][at, :] = packed[48:]
    for j, (_, matrix) in enumerate(matrices):
        high = matrix.astype(BF16).astype(F32)
        both = jnp.where(iota(matrix.shape, 1) < 64, high, pltpu.roll(matrix - high, 64, 1))
        gains[64 * j : 64 * j + 64, :] = both.astype(BF16)


def pack(blocks, experts, color, size):
    return pl.pallas_call(
        functools.partial(pack_kernel, size, color),
        out_shape=[jax.ShapeDtypeStruct((rows, size), BF16) for rows in (128, 256, 128)]
        + [jax.ShapeDtypeStruct((512, META), BF16)],
        in_specs=[pl.BlockSpec(memory_space=pltpu.SMEM)]
        + [pl.BlockSpec(memory_space=pltpu.VMEM)] * 5,
        compiler_params=PARAMS,
        cost_estimate=cost(2 * 64 * 512 * size, 2 * 1024 * size),
        name=f"pack{color}",
    )(experts, *blocks)


def turned(units):
    return [dict({a: -u[a] % RING for a in "xyz"}, c=u["c"] ^ 1) for u in units]


def moved(units, axis, offset):
    return [dict(u, **{axis: (u[axis] + offset) % RING}) for u in units]


def chunk_places(color):
    a1, a2, a3 = ORDERS[color]
    mine = [{"x": 0, "y": 0, "z": 0, "c": 0}]
    for axis in (a1, a2):
        mine = mine + moved(mine + turned(mine), axis, -1) + moved(mine, axis, 2)
    chip = mine + turned(mine)
    near = moved(chip, a3, -1)
    units = chip + near + turned(near) + moved(chip, a3, 2)
    return [(u["x"], u["y"], u["z"], u["c"]) for u in units]


def chunk_order(color):
    mine = {place: j for j, place in enumerate(chunk_places(color))}
    return [mine[place] for place in chunk_places(0)]


STEP = 512


def expert_kernel(starts, sizes, *refs):
    refs = list(refs)
    rows = [[refs.pop(0) for _ in range(4)] for _ in sizes]
    gate_ref, up_ref, down_ref = (refs.pop(0) for _ in range(3))
    outs = [[refs.pop(0) for _ in range(4)] for _ in sizes]
    held = [refs.pop(0) for _ in sizes]
    gate, up, down, part, acc, hidden, sems, out_sems = refs
    width = gate.shape[1]
    loads = []
    for k, (start, size) in enumerate(zip(starts, sizes, strict=True)):
        mine = [
            pltpu.make_async_copy(
                rows[k][i].at[pl.ds(0, 128)], held[k].at[pl.ds(128 * i, 128)], sems.at[k, i]
            )
            for i in range(4)
        ]
        span = pl.ds(start, size)
        mine.append(pltpu.make_async_copy(gate_ref.at[span], gate.at[span], sems.at[k, 4]))
        mine.append(pltpu.make_async_copy(up_ref.at[span], up.at[span], sems.at[k, 5]))
        loads.append(mine)
    downs = [
        pltpu.make_async_copy(
            down_ref.at[:, pl.ds(start, size)], down.at[:, pl.ds(start, size)], sems.at[k, 6]
        )
        for k, (start, size) in enumerate(zip(starts, sizes, strict=True))
    ]
    for load in [*loads[0], *loads[1], *loads[2], *downs]:
        load.start()
    for k, (start, size) in enumerate(zip(starts, sizes, strict=True)):
        for load in loads[k][:5]:
            load.wait()
        into = part if k else acc
        for half, weight in enumerate((gate, up)):
            if half:
                loads[k][5].wait()

            @pl.loop(0, width // 256)
            def _(n, weight=weight, half=half, into=into, k=k, start=start, size=size):
                at = pl.multiple_of(n * 256, 256)
                to = pl.multiple_of(half * width + n * 256, 256)
                into[:, pl.ds(to, 256)] = jnp.dot(
                    held[k][...],
                    weight[start : start + size, pl.ds(at, 256)],
                    preferred_element_type=F32,
                )

        if not k:
            continue
        order = chunk_order(k)
        for i in range(0, 128, 2):
            mine = jnp.concatenate([part[4 * j : 4 * j + 4, :] for j in order[i : i + 2]], axis=0)
            total = acc[4 * i : 4 * i + 8, :] + mine
            if k < 2:
                acc[4 * i : 4 * i + 8, :] = total
            else:
                gated, upped = total[:, :width], total[:, width:]
                acc[4 * i : 4 * i + 8, :width] = gated / (1.0 + jnp.exp(-gated)) * upped
    sends = []
    for k, (start, size) in enumerate(zip(starts, sizes, strict=True)):
        to_own = chunk_order(k)
        from_own = [to_own.index(j) for j in range(128)]
        for j in range(0, 128, 4):
            hidden[4 * j : 4 * j + 16, :] = jnp.concatenate(
                [acc[4 * i : 4 * i + 4, :width] for i in from_own[j : j + 4]], axis=0
            ).astype(BF16)
        downs[k].wait()
        for n in range(0, size, STEP):
            to = min(n + STEP, size)
            held[k][:, n:to] = jnp.dot(
                hidden[...], down[:, start + n : start + to], preferred_element_type=F32
            ).astype(BF16)
        for i in range(4):
            sends.append(
                pltpu.make_async_copy(
                    held[k].at[pl.ds(128 * i, 128)], outs[k][i], out_sems.at[k, i]
                )
            )
            sends[-1].start()
    for send in sends:
        send.wait()


def expert_halves(rows, gate, up, down, starts, sizes):
    width = gate.shape[1]
    everywhere = pl.BlockSpec(memory_space=pl.ANY)
    results = pl.pallas_call(
        functools.partial(expert_kernel, starts, sizes),
        out_shape=[jax.ShapeDtypeStruct((128, size), BF16) for size in sizes for _ in range(4)],
        in_specs=[everywhere] * 15,
        out_specs=[everywhere] * 12,
        scratch_shapes=[pltpu.VMEM((512, size), BF16) for size in sizes]
        + [
            pltpu.VMEM(gate.shape, BF16),
            pltpu.VMEM(up.shape, BF16),
            pltpu.VMEM(down.shape, BF16),
            pltpu.VMEM((512, 2 * width), F32),
            pltpu.VMEM((512, 2 * width), F32),
            pltpu.VMEM((512, width), BF16),
            pltpu.SemaphoreType.DMA((3, 7)),
            pltpu.SemaphoreType.DMA((3, 4)),
        ],
        compiler_params=WIDE_PARAMS,
        cost_estimate=cost(6 * 512 * gate.size, 6 * gate.size + 4 * 512 * gate.shape[0]),
        name="experts",
    )(*[ref for mine in rows for ref in mine], gate, up, down)
    return [results[4 * k : 4 * k + 4] for k in range(3)]


def weighted_block(gains_ref, back, j):
    at = slice(16 * j, 16 * j + 16)
    rows = [back[0][at, :], back[1][at, :], back[1][128 + 16 * j : 144 + 16 * j, :], back[2][at, :]]
    return jnp.dot(
        gains_ref[64 * j : 64 * j + 64, :],
        jnp.concatenate(rows + rows, axis=0),
        preferred_element_type=F32,
    )


def other_kernel(gains_ref, *refs):
    back, out = refs[:3], refs[3]
    for j in range(4):
        out[64 * j : 64 * j + 64, :] = weighted_block(gains_ref, back, 4 + j).astype(BF16)


def own_kernel(gains_ref, *refs):
    back, swapped, outs = refs[:3], refs[3], refs[4:]
    total = [
        weighted_block(gains_ref, back, j) + swapped[64 * j : 64 * j + 64, :].astype(F32)
        for j in range(4)
    ]
    outs[0][...] = total[0]
    outs[1][:64, :] = total[1].astype(BF16)
    outs[1][64:, :] = total[2].astype(BF16)
    outs[2][...] = total[3].astype(BF16)


def combine(gains, back, swapped, color, size):
    own = swapped is not None
    operands = [gains, *back, swapped] if own else [gains, *back]
    shapes = [(64, F32), (128, BF16), (64, BF16)] if own else [(256, BF16)]
    return pl.pallas_call(
        own_kernel if own else other_kernel,
        out_shape=[jax.ShapeDtypeStruct((rows, size), kind) for rows, kind in shapes],
        compiler_params=PARAMS,
        cost_estimate=cost(4 * 256 * 64 * size, 2 * 512 * size),
        name=f"{'own' if own else 'other'}{color}",
    )(*operands)


def sum_kernel(mine_ref, near_ref, far_ref, cross_ref, *outs):
    total = mine_ref[...] + near_ref[:64, :].astype(F32)
    total = total + far_ref[...].astype(F32) + cross_ref[...].astype(F32)
    outs[0][...] = total[:16]
    outs[1][...] = total[16:48].astype(BF16)
    outs[2][...] = total[48:].astype(BF16)


def sum_blocks(mine, near, far, cross, color, size):
    return pl.pallas_call(
        sum_kernel,
        out_shape=[
            jax.ShapeDtypeStruct((16, size), F32),
            jax.ShapeDtypeStruct((32, size), BF16),
            jax.ShapeDtypeStruct((16, size), BF16),
        ],
        compiler_params=PARAMS,
        cost_estimate=cost(256 * size, 1024 * size),
        name=f"sum{color}",
    )(mine, near, far, cross)


def cross_kernel(starts, sizes, *refs):
    out = refs[-1]
    for ref, start, size in zip(refs, starts, sizes, strict=False):
        out[:, start : start + size] = ref[16:, :]


def cross_rows(near, starts, sizes, rows, width):
    return pl.pallas_call(
        functools.partial(cross_kernel, starts, sizes),
        out_shape=jax.ShapeDtypeStruct((rows, width), BF16),
        compiler_params=PARAMS,
        cost_estimate=cost(0, 4 * rows * width),
        name="cross",
    )(*near)


def finish_kernel(starts, sizes, crossed_ref, *refs):
    out = refs[-1]
    for k, (start, size) in enumerate(zip(starts, sizes, strict=True)):
        mine, near, far = refs[3 * k : 3 * k + 3]
        at = slice(start, start + size)
        total = mine[...] + near[:16, :].astype(F32) + far[...].astype(F32)
        out[:, at] = (total + crossed_ref[:, at].astype(F32)).astype(BF16)


def finish(crossed, pieces, starts, sizes, rows, width):
    return pl.pallas_call(
        functools.partial(finish_kernel, starts, sizes),
        out_shape=jax.ShapeDtypeStruct((rows, width), BF16),
        compiler_params=PARAMS,
        cost_estimate=cost(4 * rows * width, 10 * rows * width),
        name="finish",
    )(crossed, *pieces)


COLORS = range(3)


def after(value, earlier):
    return lax.optimization_barrier((value, earlier))


def body(tokens, routes, route_weight, gate_weight, up_weight, down_weight):
    micro, count, width = tokens.shape
    rows = micro * count
    choices = routes.shape[2]
    starts, sizes = column_split(width)
    node, local = lax.axis_index("node"), lax.axis_index("local")
    here = {"z": node // 2, "c": node % 2, "x": local // 4, "y": local % 4}
    sign = 1 - 2 * here["c"]

    def expert_at(axis, offset, core):
        place = dict(here)
        place[axis] = (here[axis] + sign * offset) % RING
        place["c"] = (here["c"] + core) % 2
        return (place["z"] * 2 + place["c"]) * 8 + (place["x"] * 4 + place["y"]) // 2

    groups = ((0, 0), (1, 0), (1, 1), (2, 0))
    experts = jnp.stack(
        [jnp.stack([expert_at(order[2], *group) for group in groups]) for order in ORDERS]
    ).astype(jnp.int32)
    gains = route_weight.reshape(rows, choices)
    info = jnp.concatenate(
        [
            routes.reshape(rows, choices).astype(F32),
            gains,
            gains,
            jnp.zeros((rows, META - 3 * choices), F32),
        ],
        axis=1,
    )
    flat = tokens.reshape(rows, width)
    prepared = prepare(
        flat, info, from_offset(flat, "c", 1), from_offset(info, "c", 1), starts, sizes
    )
    chip, mine = prepared[:3], prepared[3:]

    near = [from_offset(chip[k], ORDERS[k][0], -1) for k in COLORS]
    far = [from_offset(mine[k], ORDERS[k][0], 2) for k in COLORS]
    near, far = after(near, far)
    mine = [jnp.concatenate([mine[k], near[k], far[k]], axis=0) for k in COLORS]
    far = [from_offset(mine[k], ORDERS[k][1], 2) for k in COLORS]
    theirs = [from_offset(mine[k], "c", 1) for k in COLORS]
    chip = [jnp.concatenate([mine[k], theirs[k]], axis=0) for k in COLORS]
    chip, far = after(chip, far)
    near = [from_offset(chip[k], ORDERS[k][1], -1) for k in COLORS]
    their_far = [from_offset(far[k], "c", 1) for k in COLORS]
    near, their_far = after(near, their_far)
    their_near = [from_offset(near[k], "c", 1) for k in COLORS]
    blocks = [[chip[k], near[k], far[k], their_near[k], their_far[k]] for k in COLORS]
    packed = [pack(blocks[k], experts, k, sizes[k]) for k in COLORS]
    near = [from_offset(packed[k][1], ORDERS[k][2], -1) for k in COLORS]
    far = [packed[k][2] for k in COLORS]
    for k in COLORS:
        far[k], near[k] = after(far[k], near[k])
    far = [from_offset(far[k], ORDERS[k][2], 2) for k in COLORS]
    crossed = [from_offset(near[k][128:], "c", 1) for k in COLORS]

    landed = [[packed[k][0], near[k], crossed[k], far[k]] for k in COLORS]
    outs = expert_halves(
        landed, gate_weight[0], up_weight[0], down_weight[0], starts, sizes
    )

    crossed = [from_offset(outs[k][2], "c", 1) for k in COLORS]
    far = [from_offset(outs[k][3], ORDERS[k][2], 2) for k in COLORS]
    near = [jnp.concatenate([outs[k][1], crossed[k]], axis=0) for k in COLORS]
    near = [from_offset(near[k], ORDERS[k][2], 1) for k in COLORS]
    back = [[outs[k][0], near[k], far[k]] for k in COLORS]
    theirs = [combine(packed[k][3], back[k], None, k, sizes[k])[0] for k in COLORS]
    swapped = [from_offset(theirs[k], "c", 1) for k in COLORS]
    sums = [combine(packed[k][3], back[k], swapped[k], k, sizes[k]) for k in COLORS]
    near = [from_offset(sums[k][1], ORDERS[k][1], 1) for k in COLORS]
    far = [sums[k][2] for k in COLORS]
    for k in COLORS:
        far[k], near[k] = after(far[k], near[k])
    far = [from_offset(far[k], ORDERS[k][1], 2) for k in COLORS]
    crossed = [from_offset(near[k][64:], "c", 1) for k in COLORS]
    parts = [sum_blocks(sums[k][0], near[k], far[k], crossed[k], k, sizes[k]) for k in COLORS]
    near = [from_offset(parts[k][1], ORDERS[k][0], 1) for k in COLORS]
    far = [from_offset(parts[k][2], ORDERS[k][0], 2) for k in COLORS]
    crossed = from_offset(cross_rows(near, starts, sizes, rows, width), "c", 1)
    pieces = []
    for k in COLORS:
        pieces += [parts[k][0], near[k], far[k]]
    return finish(crossed, pieces, starts, sizes, rows, width).reshape(micro, count, width)


def solution(mesh):
    placed = (
        P(None, AXES, None),
        P(None, AXES, None),
        P(None, AXES, None),
        P(AXES, None, None),
        P(AXES, None, None),
        P(AXES, None, None),
    )
    return jax.shard_map(
        body,
        mesh=mesh,
        in_specs=placed,
        out_specs=P(None, AXES, None),
        check_vma=False,
    )
```

profile of v0, /device:TPU:0, one launch (start us, length us, event | category | flops | bytes accessed | tf_op | source)
XLA Modules:
  0.0 203.6 jit_solution(16188051809962207238)
XLA Ops:
  0.8 0.8 maximum_maximum_fusion.info_ref
  2.2 0.8 collective-permute-done.1.info2_ref
  3.0 0.9 copy-done.12
  4.0 4.0 %collective-permute-start.7 = (bf16[16,2432]{1,0:T(8,128)(2,1)S(1)}, bf16[16,2432]{1,0:T(8,128)(2,1)S(1)}, u32[]{:S(2)}, u32[]{:S(2)}) collective-permute-start(bf16[16,2432]{1,0:T(8,128)(2,1)S(1)} %get-tuple-element.88), channel_id=1, source_target_pairs={{0,64},{1,65},{2,66},{3,67},{4,68},{5,69},{6,70},{7,71},{8,72},{9,... | collective-permute-start | bytes 233480 | tf_op jit(solution)/shard_map/ppermute | solution.py:41
  8.0 3.0 %collective-permute-start.5 = (bf16[16,2560]{1,0:T(8,128)(2,1)S(1)}, bf16[16,2560]{1,0:T(8,128)(2,1)S(1)}, u32[]{:S(2)}, u32[]{:S(2)}) collective-permute-start(bf16[16,2560]{1,0:T(8,128)(2,1)S(1)} %get-tuple-element.83), channel_id=1, source_target_pairs={{0,8},{1,9},{2,10},{3,11},{4,12},{5,13},{6,14},{7,15},{8,0},{9,1},... | collective-permute-start | bytes 245768 | tf_op jit(solution)/shard_map/ppermute | solution.py:41
  11.0 3.2 %collective-permute-start.6 = (bf16[16,2560]{1,0:T(8,128)(2,1)S(1)}, bf16[16,2560]{1,0:T(8,128)(2,1)S(1)}, u32[]{:S(2)}, u32[]{:S(2)}) collective-permute-start(bf16[16,2560]{1,0:T(8,128)(2,1)S(1)} %get-tuple-element.87), channel_id=1, source_target_pairs={{0,2},{1,3},{2,0},{3,1},{4,6},{5,7},{6,4},{7,5},{8,10},{9,11},{10,... | collective-permute-start | bytes 245768 | tf_op jit(solution)/shard_map/ppermute | solution.py:41
  14.3 1.1 collective-permute-start.4
  17.0 3.8 %collective-permute-done.4 = bf16[32,2432]{1,0:T(8,128)(2,1)S(1)} collective-permute-done((bf16[32,2432]{1,0:T(8,128)(2,1)S(1)}, bf16[32,2432]{1,0:T(8,128)(2,1)S(1)}, u32[]{:S(2)}, u32[]{:S(2)}) %collective-permute-start.4) | collective-permute-done | bytes 155680 | tf_op jit(solution)/shard_map/ppermute | solution.py:41
  20.8 1.1 collective-permute-done.2
  22.5 2.1 %collective-permute-start.13 = (bf16[64,2432]{1,0:T(8,128)(2,1)S(1)}, bf16[64,2432]{1,0:T(8,128)(2,1)S(1)}, u32[]{:S(2)}, u32[]{:S(2)}) collective-permute-start(bf16[64,2432]{1,0:T(8,128)(2,1)S(1)} %constant_dynamic-update-slice_fusion.6), channel_id=1, source_target_pairs={{0,8},{1,9},{2,10},{3,11},{4,12},{5,13},{6,14},{7,15},{8,0},{9,1},... | collective-permute-start | bytes 933896 | tf_op jit(solution)/shard_map/ppermute | solution.py:41
  24.6 1.2 collective-permute-start.12
  26.7 0.8 collective-permute-done.9
  28.0 3.0 %collective-permute-done.13.refs_2_ = bf16[64,2432]{1,0:T(8,128)(2,1)S(1)} collective-permute-done((bf16[64,2432]{1,0:T(8,128)(2,1)S(1)}, bf16[64,2432]{1,0:T(8,128)(2,1)S(1)}, u32[]{:S(2)}, u32[]{:S(2)}) %collective-permute-start.13) | collective-permute-done | bytes 311328 | tf_op jit(solution)/shard_map/ppermute | solution.py:41
  31.0 5.3 %collective-permute-done.12.refs_2_ = bf16[64,2560]{1,0:T(8,128)(2,1)S(1)} collective-permute-done((bf16[64,2560]{1,0:T(8,128)(2,1)S(1)}, bf16[64,2560]{1,0:T(8,128)(2,1)S(1)}, u32[]{:S(2)}, u32[]{:S(2)}) %collective-permute-start.12) | collective-permute-done | bytes 327712 | tf_op jit(solution)/shard_map/ppermute | solution.py:41
  36.3 1.3 collective-permute-done.11.refs_2_
  37.6 1.9 collective-permute-start.15
  39.5 1.5 collective-permute-start.16
  41.0 0.7 copy-done.2
  43.0 0.7 copy-done.4
  43.7 0.7 copy-done.6
  44.5 0.7 copy-done.8
  45.2 5.9 %collective-permute-done.16.refs_1_ = bf16[128,2432]{1,0:T(8,128)(2,1)} collective-permute-done((bf16[128,2432]{1,0:T(8,128)(2,1)S(1)}, bf16[128,2432]{1,0:T(8,128)(2,1)}, u32[]{:S(2)}, u32[]{:S(2)}) %collective-permute-start.16) | collective-permute-done | bytes 622624 | tf_op jit(solution)/shard_map/ppermute | solution.py:41
  52.2 1.3 collective-permute-done.28.refs_3_
  53.5 1.0 copy-done.11
  54.5 2.6 %pack2.1 = (bf16[128,2304]{1,0:T(8,128)(2,1)S(1)}, bf16[256,2304]{1,0:T(8,128)(2,1)S(1)}, bf16[128,2304]{1,0:T(8,128)(2,1)S(1)}, bf16[512,128]{1,0:T(8,128)(2,1)S(1)}) custom-call(s32[3,4]{1,0:T(4,128)S(1)} %pad_add_fusion.experts_ref, bf16[128,2432]{1,0:T(8,128)(2,1)S(1)} %pad_maximum_fusion.5.refs_0_, bf16[128,2432]{1,0:T(8,128)(2,1)} %collective-permute-done.16.refs_1_, ...), custom_call_target="tpu_custom_call" | custom-call | flops 150994944 | bytes 4718592 | tf_op jit(solution)/shard_map/pack2/pallas_call | solution.py:146
  57.0 0.8 copy-done.15
  58.5 1.9 pack1.1
  60.9 1.9 pack0.1
  62.9 0.9 collective-permute-start.21
  63.8 11.5 %collective-permute-done.29.refs_9_ = bf16[256,2304]{1,0:T(8,128)(2,1)S(1)} collective-permute-done((bf16[256,2304]{1,0:T(8,128)(2,1)S(1)}, bf16[256,2304]{1,0:T(8,128)(2,1)S(1)}, u32[]{:S(2)}, u32[]{:S(2)}) %collective-permute-start.29) | collective-permute-done | bytes 1179680 | tf_op jit(solution)/shard_map/ppermute | solution.py:41
  75.4 3.3 %collective-permute-done.25.refs_5_ = bf16[256,2432]{1,0:T(8,128)(2,1)S(1)} collective-permute-done((bf16[256,2432]{1,0:T(8,128)(2,1)S(1)}, bf16[256,2432]{1,0:T(8,128)(2,1)S(1)}, u32[]{:S(2)}, u32[]{:S(2)}) %collective-permute-start.25) | collective-permute-done | bytes 1245216 | tf_op jit(solution)/shard_map/ppermute | solution.py:41
  79.6 1.4 collective-permute-done.21.refs_1_
  81.3 1.2 collective-permute-start.23
  82.5 3.0 %collective-permute-start.31 = (bf16[128,2304]{1,0:T(8,128)(2,1)S(1)}, bf16[128,2304]{1,0:T(8,128)(2,1)S(1)}, u32[]{:S(2)}, u32[]{:S(2)}) collective-permute-start(bf16[128,2304]{1,0:T(8,128)(2,1)S(1)} %get-tuple-element.122), channel_id=1, source_target_pairs={{0,2},{1,3},{2,0},{3,1},{4,6},{5,7},{6,4},{7,5},{8,10},{9,11},{10,... | collective-permute-start | bytes 1769480 | tf_op jit(solution)/shard_map/ppermute | solution.py:41
  85.5 13.9 %collective-permute-done.31.refs_11_ = bf16[128,2304]{1,0:T(8,128)(2,1)S(1)} collective-permute-done((bf16[128,2304]{1,0:T(8,128)(2,1)S(1)}, bf16[128,2304]{1,0:T(8,128)(2,1)S(1)}, u32[]{:S(2)}, u32[]{:S(2)}) %collective-permute-start.31) | collective-permute-done | bytes 589856 | tf_op jit(solution)/shard_map/ppermute | solution.py:41
  99.5 0.8 copy-done.27
  101.1 19.8 %experts.1 = (bf16[128,2432]{1,0:T(8,128)(2,1)}, bf16[128,2432]{1,0:T(8,128)(2,1)}, bf16[128,2432]{1,0:T(8,128)(2,1)}, bf16[128,2432]{1,0:T(8,128)(2,1)}, bf16[1...) custom-call(bf16[128,2432]{1,0:T(8,128)(2,1)} %copy-done.14, ...), custom_call_target="tpu_custom_call" | custom-call | flops 11274289152 | bytes 36700160 | tf_op jit(solution)/shard_map/experts/pallas_call | solution.py:270
  121.8 2.6 %collective-permute-start.42 = (bf16[128,2432]{1,0:T(8,128)(2,1)}, bf16[128,2432]{1,0:T(8,128)(2,1)S(1)}, u32[]{:S(2)}, u32[]{:S(2)}) collective-permute-start(bf16[128,2432]{1,0:T(8,128)(2,1)} %get-tuple-element.137), channel_id=1, source_target_pairs={{0,8},{1,9},{2,10},{3,11},{4,12},{5,13},{6,14},{7,15},{8,0},{9,1},... | collective-permute-start | bytes 1867784 | tf_op jit(solution)/shard_map/ppermute | solution.py:41
  124.4 1.2 pad_maximum_fusion.1
  125.7 2.0 collective-permute-start.41
  127.8 1.6 collective-permute-start.33
  129.5 1.9 collective-permute-start.49
  131.4 1.7 collective-permute-start.34
  133.1 7.3 %collective-permute-done.42.refs_2_ = bf16[128,2432]{1,0:T(8,128)(2,1)S(1)} collective-permute-done((bf16[128,2432]{1,0:T(8,128)(2,1)}, bf16[128,2432]{1,0:T(8,128)(2,1)S(1)}, u32[]{:S(2)}, u32[]{:S(2)}) %collective-permute-start.42) | collective-permute-done | bytes 622624 | tf_op jit(solution)/shard_map/ppermute | solution.py:41
  140.4 3.2 %collective-permute-start.50 = (bf16[128,2304]{1,0:T(8,128)(2,1)S(1)}, bf16[128,2304]{1,0:T(8,128)(2,1)S(1)}, u32[]{:S(2)}, u32[]{:S(2)}) collective-permute-start(bf16[128,2304]{1,0:T(8,128)(2,1)S(1)} %copy-done.25), channel_id=1, source_target_pairs={{0,2},{1,3},{2,0},{3,1},{4,6},{5,7},{6,4},{7,5},{8,10},{9,11},{10,... | collective-permute-start | bytes 1769480 | tf_op jit(solution)/shard_map/ppermute | solution.py:41
  143.6 9.9 %collective-permute-done.41.refs_1_ = bf16[256,2432]{1,0:T(8,128)(2,1)S(1)} collective-permute-done((bf16[256,2432]{1,0:T(8,128)(2,1)S(1)}, bf16[256,2432]{1,0:T(8,128)(2,1)S(1)}, u32[]{:S(2)}, u32[]{:S(2)}) %collective-permute-start.41) | collective-permute-done | bytes 1245216 | tf_op jit(solution)/shard_map/ppermute | solution.py:41
  155.1 3.0 %collective-permute-start.35 = (bf16[256,2432]{1,0:T(8,128)(2,1)S(1)}, bf16[256,2432]{1,0:T(8,128)(2,1)S(1)}, u32[]{:S(2)}, u32[]{:S(2)}) collective-permute-start(bf16[256,2432]{1,0:T(8,128)(2,1)S(1)} %other0.1), channel_id=1, source_target_pairs={{0,16},{1,17},{2,18},{3,19},{4,20},{5,21},{6,22},{7,23},{8,24},{9,... | collective-permute-start | bytes 3735560 | tf_op jit(solution)/shard_map/ppermute | solution.py:41
  159.2 3.9 %collective-permute-start.44 = (bf16[128,2432]{1,0:T(8,128)(2,1)S(1)}, bf16[128,2432]{1,0:T(8,128)(2,1)S(1)}, u32[]{:S(2)}, u32[]{:S(2)}) collective-permute-start(bf16[128,2432]{1,0:T(8,128)(2,1)S(1)} %get-tuple-element.140), channel_id=1, source_target_pairs={{0,96},{1,97},{2,98},{3,99},{4,100},{5,101},{6,102},{7,103},{8,104... | collective-permute-start | bytes 1867784 | tf_op jit(solution)/shard_map/ppermute | solution.py:41
  163.6 1.9 collective-permute-start.36
  166.5 4.7 %collective-permute-done.44.near_ref = bf16[128,2432]{1,0:T(8,128)(2,1)S(1)} collective-permute-done((bf16[128,2432]{1,0:T(8,128)(2,1)S(1)}, bf16[128,2432]{1,0:T(8,128)(2,1)S(1)}, u32[]{:S(2)}, u32[]{:S(2)}) %collective-permute-start.44) | collective-permute-done | bytes 622624 | tf_op jit(solution)/shard_map/ppermute | solution.py:41
  171.3 1.7 collective-permute-start.45
  173.0 0.9 collective-permute-done.36.near_ref
  174.0 3.3 %collective-permute-start.37 = (bf16[64,2432]{1,0:T(8,128)(2,1)S(1)}, bf16[64,2432]{1,0:T(8,128)(2,1)S(1)}, u32[]{:S(2)}, u32[]{:S(2)}) collective-permute-start(bf16[64,2432]{1,0:T(8,128)(2,1)S(1)} %get-tuple-element.131), channel_id=1, source_target_pairs={{0,2},{1,3},{2,0},{3,1},{4,6},{5,7},{6,4},{7,5},{8,10},{9,11},{10,... | collective-permute-start | bytes 933896 | tf_op jit(solution)/shard_map/ppermute | solution.py:41
  177.6 1.3 collective-permute-start.53
  178.9 3.6 %collective-permute-done.45.far_ref = bf16[64,2432]{1,0:T(8,128)(2,1)S(1)} collective-permute-done((bf16[64,2432]{1,0:T(8,128)(2,1)S(1)}, bf16[64,2432]{1,0:T(8,128)(2,1)S(1)}, u32[]{:S(2)}, u32[]{:S(2)}) %collective-permute-start.45) | collective-permute-done | bytes 311328 | tf_op jit(solution)/shard_map/ppermute | solution.py:41
  182.7 2.1 %collective-permute-start.47 = (bf16[32,2432]{1,0:T(8,128)(2,1)S(1)}, bf16[32,2432]{1,0:T(8,128)(2,1)S(1)}, u32[]{:S(2)}, u32[]{:S(2)}) collective-permute-start(bf16[32,2432]{1,0:T(8,128)(2,1)S(1)} %get-tuple-element.143), channel_id=1, source_target_pairs={{0,3},{1,0},{2,1},{3,2},{4,7},{5,4},{6,5},{7,6},{8,11},{9,8},{10,9... | collective-permute-start | bytes 466952 | tf_op jit(solution)/shard_map/ppermute | solution.py:41
  185.9 3.0 %collective-permute-done.53.far_ref = bf16[64,2304]{1,0:T(8,128)(2,1)S(1)} collective-permute-done((bf16[64,2304]{1,0:T(8,128)(2,1)S(1)}, bf16[64,2304]{1,0:T(8,128)(2,1)S(1)}, u32[]{:S(2)}, u32[]{:S(2)}) %collective-permute-start.53) | collective-permute-done | bytes 294944 | tf_op jit(solution)/shard_map/ppermute | solution.py:41
  189.1 2.2 %collective-permute-start.55 = (bf16[32,2304]{1,0:T(8,128)(2,1)S(1)}, bf16[32,2304]{1,0:T(8,128)(2,1)S(1)}, u32[]{:S(2)}, u32[]{:S(2)}) collective-permute-start(bf16[32,2304]{1,0:T(8,128)(2,1)S(1)} %get-tuple-element.154), channel_id=1, source_target_pairs={{0,96},{1,97},{2,98},{3,99},{4,100},{5,101},{6,102},{7,103},{8,104... | collective-permute-start | bytes 442376 | tf_op jit(solution)/shard_map/ppermute | solution.py:41
  191.3 3.0 %collective-permute-done.55.refs_2_.refs_7_ = bf16[32,2304]{1,0:T(8,128)(2,1)S(1)} collective-permute-done((bf16[32,2304]{1,0:T(8,128)(2,1)S(1)}, bf16[32,2304]{1,0:T(8,128)(2,1)S(1)}, u32[]{:S(2)}, u32[]{:S(2)}) %collective-permute-start.55) | collective-permute-done | bytes 147488 | tf_op jit(solution)/shard_map/ppermute | solution.py:41
  194.4 0.8 collective-permute-start.58
  195.2 1.7 collective-permute-start.57
  196.9 1.4 collective-permute-start.59
  198.3 4.5 %collective-permute-done.59.refs_8_ = bf16[16,2304]{1,0:T(8,128)(2,1)S(1)} collective-permute-done((bf16[16,2304]{1,0:T(8,128)(2,1)S(1)}, bf16[16,2304]{1,0:T(8,128)(2,1)S(1)}, u32[]{:S(2)}, u32[]{:S(2)}) %collective-permute-start.59) | collective-permute-done | bytes 73760 | tf_op jit(solution)/shard_map/ppermute | solution.py:41
  202.8 0.8 finish.1
  (155 shorter events, 17.4 us)
Async XLA Ops:
  0.0 3.0 %collective-permute-start = (bf16[16,7168]{1,0:T(8,128)(2,1)}, bf16[16,7168]{1,0:T(8,128)(2,1)S(1)}, u32[]{:S(2)}, u32[]{:S(2)}) collective-permute-start(bf16[16,7168]{1,0:T(8,128)(2,1)} %bitcast.26), channel_id=1, source_target_pairs={{0,16},{1,17},{2,18},{3,19},{4,20},{5,21},{6,22},{7,23},{8,24},{9,... | collective-permute-start | bytes 688136 | tf_op jit(solution)/shard_map/ppermute | solution.py:41
  1.6 1.4 collective-permute-start.1
  4.0 12.0 %collective-permute-start.7 = (bf16[16,2432]{1,0:T(8,128)(2,1)S(1)}, bf16[16,2432]{1,0:T(8,128)(2,1)S(1)}, u32[]{:S(2)}, u32[]{:S(2)}) collective-permute-start(bf16[16,2432]{1,0:T(8,128)(2,1)S(1)} %get-tuple-element.88), channel_id=1, source_target_pairs={{0,64},{1,65},{2,66},{3,67},{4,68},{5,69},{6,70},{7,71},{8,72},{9,... | collective-permute-start | bytes 233480 | tf_op jit(solution)/shard_map/ppermute | solution.py:41
  8.0 8.6 %collective-permute-start.5 = (bf16[16,2560]{1,0:T(8,128)(2,1)S(1)}, bf16[16,2560]{1,0:T(8,128)(2,1)S(1)}, u32[]{:S(2)}, u32[]{:S(2)}) collective-permute-start(bf16[16,2560]{1,0:T(8,128)(2,1)S(1)} %get-tuple-element.83), channel_id=1, source_target_pairs={{0,8},{1,9},{2,10},{3,11},{4,12},{5,13},{6,14},{7,15},{8,0},{9,1},... | collective-permute-start | bytes 245768 | tf_op jit(solution)/shard_map/ppermute | solution.py:41
  11.0 5.9 %collective-permute-start.6 = (bf16[16,2560]{1,0:T(8,128)(2,1)S(1)}, bf16[16,2560]{1,0:T(8,128)(2,1)S(1)}, u32[]{:S(2)}, u32[]{:S(2)}) collective-permute-start(bf16[16,2560]{1,0:T(8,128)(2,1)S(1)} %get-tuple-element.87), channel_id=1, source_target_pairs={{0,2},{1,3},{2,0},{3,1},{4,6},{5,7},{6,4},{7,5},{8,10},{9,11},{10,... | collective-permute-start | bytes 245768 | tf_op jit(solution)/shard_map/ppermute | solution.py:41
  14.3 6.5 %collective-permute-start.4 = (bf16[32,2432]{1,0:T(8,128)(2,1)S(1)}, bf16[32,2432]{1,0:T(8,128)(2,1)S(1)}, u32[]{:S(2)}, u32[]{:S(2)}) collective-permute-start(bf16[32,2432]{1,0:T(8,128)(2,1)S(1)} %get-tuple-element.86), channel_id=1, source_target_pairs={{0,32},{1,33},{2,34},{3,35},{4,36},{5,37},{6,38},{7,39},{8,40},{9,... | collective-permute-start | bytes 466952 | tf_op jit(solution)/shard_map/ppermute | solution.py:41
  15.3 6.5 %collective-permute-start.2 = (bf16[32,2560]{1,0:T(8,128)(2,1)S(1)}, bf16[32,2560]{1,0:T(8,128)(2,1)S(1)}, u32[]{:S(2)}, u32[]{:S(2)}) collective-permute-start(bf16[32,2560]{1,0:T(8,128)(2,1)S(1)} %get-tuple-element.84), channel_id=1, source_target_pairs={{0,4},{1,5},{2,6},{3,7},{4,8},{5,9},{6,10},{7,11},{8,12},{9,13},{1... | collective-permute-start | bytes 491528 | tf_op jit(solution)/shard_map/ppermute | solution.py:41
  15.9 6.5 %collective-permute-start.3 = (bf16[32,2560]{1,0:T(8,128)(2,1)S(1)}, bf16[32,2560]{1,0:T(8,128)(2,1)S(1)}, u32[]{:S(2)}, u32[]{:S(2)}) collective-permute-start(bf16[32,2560]{1,0:T(8,128)(2,1)S(1)} %get-tuple-element.85), channel_id=1, source_target_pairs={{0,1},{1,2},{2,3},{3,0},{4,5},{5,6},{6,7},{7,4},{8,9},{9,10},{10,1... | collective-permute-start | bytes 491528 | tf_op jit(solution)/shard_map/ppermute | solution.py:41
  22.5 8.5 %collective-permute-start.13 = (bf16[64,2432]{1,0:T(8,128)(2,1)S(1)}, bf16[64,2432]{1,0:T(8,128)(2,1)S(1)}, u32[]{:S(2)}, u32[]{:S(2)}) collective-permute-start(bf16[64,2432]{1,0:T(8,128)(2,1)S(1)} %constant_dynamic-update-slice_fusion.6), channel_id=1, source_target_pairs={{0,8},{1,9},{2,10},{3,11},{4,12},{5,13},{6,14},{7,15},{8,0},{9,1},... | collective-permute-start | bytes 933896 | tf_op jit(solution)/shard_map/ppermute | solution.py:41
  24.6 1.7 collective-permute-start.10
  24.6 11.7 %collective-permute-start.12 = (bf16[64,2560]{1,0:T(8,128)(2,1)S(1)}, bf16[64,2560]{1,0:T(8,128)(2,1)S(1)}, u32[]{:S(2)}, u32[]{:S(2)}) collective-permute-start(bf16[64,2560]{1,0:T(8,128)(2,1)S(1)} %constant_dynamic-update-slice_fusion.3), channel_id=1, source_target_pairs={{0,64},{1,65},{2,66},{3,67},{4,68},{5,69},{6,70},{7,71},{8,72},{9,... | collective-permute-start | bytes 983048 | tf_op jit(solution)/shard_map/ppermute | solution.py:41
  25.9 1.6 collective-permute-start.9
  26.1 11.5 %collective-permute-start.11 = (bf16[64,2560]{1,0:T(8,128)(2,1)S(1)}, bf16[64,2560]{1,0:T(8,128)(2,1)S(1)}, u32[]{:S(2)}, u32[]{:S(2)}) collective-permute-start(bf16[64,2560]{1,0:T(8,128)(2,1)S(1)} %constant_dynamic-update-slice_fusion), channel_id=1, source_target_pairs={{0,2},{1,3},{2,0},{3,1},{4,6},{5,7},{6,4},{7,5},{8,10},{9,11},{10,... | collective-permute-start | bytes 983048 | tf_op jit(solution)/shard_map/ppermute | solution.py:41
  26.3 1.7 collective-permute-start.8
  37.6 13.5 %collective-permute-start.14 = (bf16[128,2560]{1,0:T(8,128)(2,1)S(1)}, bf16[128,2560]{1,0:T(8,128)(2,1)S(1)}, u32[]{:S(2)}, u32[]{:S(2)}) collective-permute-start(bf16[128,2560]{1,0:T(8,128)(2,1)S(1)} %pad_maximum_fusion.3.refs_0_), channel_id=1, source_target_pairs={{0,1},{1,2},{2,3},{3,0},{4,5},{5,6},{6,7},{7,4},{8,9},{9,10},{10,1... | collective-permute-start | bytes 1966088 | tf_op jit(solution)/shard_map/ppermute | solution.py:41
  37.6 13.5 %collective-permute-start.15 = (bf16[128,2560]{1,0:T(8,128)(2,1)S(1)}, bf16[128,2560]{1,0:T(8,128)(2,1)S(1)}, u32[]{:S(2)}, u32[]{:S(2)}) collective-permute-start(bf16[128,2560]{1,0:T(8,128)(2,1)S(1)} %pad_maximum_fusion.4.refs_0_), channel_id=1, source_target_pairs={{0,32},{1,33},{2,34},{3,35},{4,36},{5,37},{6,38},{7,39},{8,40},{9,... | collective-permute-start | bytes 1966088 | tf_op jit(solution)/shard_map/ppermute | solution.py:41
  39.5 2.2 %collective-permute-start.19 = (bf16[64,2432]{1,0:T(8,128)(2,1)S(1)}, bf16[64,2432]{1,0:T(8,128)(2,1)S(1)}, u32[]{:S(2)}, u32[]{:S(2)}) collective-permute-start(bf16[64,2432]{1,0:T(8,128)(2,1)S(1)} %collective-permute-done.13.refs_2_), channel_id=1, source_target_pairs={{0,16},{1,17},{2,18},{3,19},{4,20},{5,21},{6,22},{7,23},{8,24},{9,... | collective-permute-start | bytes 933896 | tf_op jit(solution)/shard_map/ppermute | solution.py:41
  39.5 11.6 %collective-permute-start.16 = (bf16[128,2432]{1,0:T(8,128)(2,1)S(1)}, bf16[128,2432]{1,0:T(8,128)(2,1)}, u32[]{:S(2)}, u32[]{:S(2)}) collective-permute-start(bf16[128,2432]{1,0:T(8,128)(2,1)S(1)} %pad_maximum_fusion.5.refs_0_), channel_id=1, source_target_pairs={{0,4},{1,5},{2,6},{3,7},{4,8},{5,9},{6,10},{7,11},{8,12},{9,13},{1... | collective-permute-start | bytes 1867784 | tf_op jit(solution)/shard_map/ppermute | solution.py:41
  41.0 2.7 %collective-permute-start.17 = (bf16[64,2560]{1,0:T(8,128)(2,1)S(1)}, bf16[64,2560]{1,0:T(8,128)(2,1)S(1)}, u32[]{:S(2)}, u32[]{:S(2)}) collective-permute-start(bf16[64,2560]{1,0:T(8,128)(2,1)S(1)} %collective-permute-done.11.refs_2_), channel_id=1, source_target_pairs={{0,16},{1,17},{2,18},{3,19},{4,20},{5,21},{6,22},{7,23},{8,24},{9,... | collective-permute-start | bytes 983048 | tf_op jit(solution)/shard_map/ppermute | solution.py:41
  42.5 2.0 collective-permute-start.18
  51.1 2.4 %collective-permute-start.28 = (bf16[128,2432]{1,0:T(8,128)(2,1)}, bf16[128,2432]{1,0:T(8,128)(2,1)}, u32[]{:S(2)}, u32[]{:S(2)}) collective-permute-start(bf16[128,2432]{1,0:T(8,128)(2,1)} %collective-permute-done.16.refs_1_), channel_id=1, source_target_pairs={{0,16},{1,17},{2,18},{3,19},{4,20},{5,21},{6,22},{7,23},{8,24},{9,... | collective-permute-start | bytes 1867784 | tf_op jit(solution)/shard_map/ppermute | solution.py:41
  51.6 9.3 %collective-permute-start.20 = (bf16[128,2560]{1,0:T(8,128)(2,1)S(1)}, bf16[128,2560]{1,0:T(8,128)(2,1)S(1)}, u32[]{:S(2)}, u32[]{:S(2)}) collective-permute-start(bf16[128,2560]{1,0:T(8,128)(2,1)S(1)} %collective-permute-done.14.refs_1_), channel_id=1, source_target_pairs={{0,16},{1,17},{2,18},{3,19},{4,20},{5,21},{6,22},{7,23},{8,24},{9,... | collective-permute-start | bytes 1966088 | tf_op jit(solution)/shard_map/ppermute | solution.py:41
  51.7 6.8 %collective-permute-start.24 = (bf16[128,2560]{1,0:T(8,128)(2,1)S(1)}, bf16[128,2560]{1,0:T(8,128)(2,1)S(1)}, u32[]{:S(2)}, u32[]{:S(2)}) collective-permute-start(bf16[128,2560]{1,0:T(8,128)(2,1)S(1)} %collective-permute-done.15.refs_1_), channel_id=1, source_target_pairs={{0,16},{1,17},{2,18},{3,19},{4,20},{5,21},{6,22},{7,23},{8,24},{9,... | collective-permute-start | bytes 1966088 | tf_op jit(solution)/shard_map/ppermute | solution.py:41
  57.9 17.4 %collective-permute-start.29 = (bf16[256,2304]{1,0:T(8,128)(2,1)S(1)}, bf16[256,2304]{1,0:T(8,128)(2,1)S(1)}, u32[]{:S(2)}, u32[]{:S(2)}) collective-permute-start(bf16[256,2304]{1,0:T(8,128)(2,1)S(1)} %get-tuple-element.120), channel_id=1, source_target_pairs={{0,1},{1,2},{2,3},{3,0},{4,5},{5,6},{6,7},{7,4},{8,9},{9,10},{10,1... | collective-permute-start | bytes 3538952 | tf_op jit(solution)/shard_map/ppermute | solution.py:41
  60.4 18.4 %collective-permute-start.25 = (bf16[256,2432]{1,0:T(8,128)(2,1)S(1)}, bf16[256,2432]{1,0:T(8,128)(2,1)S(1)}, u32[]{:S(2)}, u32[]{:S(2)}) collective-permute-start(bf16[256,2432]{1,0:T(8,128)(2,1)S(1)} %get-tuple-element.113), channel_id=1, source_target_pairs={{0,4},{1,5},{2,6},{3,7},{4,8},{5,9},{6,10},{7,11},{8,12},{9,13},{1... | collective-permute-start | bytes 3735560 | tf_op jit(solution)/shard_map/ppermute | solution.py:41
  62.8 18.2 %copy-start.14 = (bf16[128,2432]{1,0:T(8,128)(2,1)}, bf16[128,2432]{1,0:T(8,128)(2,1)S(1)}, u32[]{:S(2)}) copy-start(bf16[128,2432]{1,0:T(8,128)(2,1)S(1)} %get-tuple-element.104.refs_0_) | copy-start | bytes 1867780
  62.9 18.2 %collective-permute-start.21 = (bf16[256,2432]{1,0:T(8,128)(2,1)S(1)}, bf16[256,2432]{1,0:T(8,128)(2,1)S(1)}, u32[]{:S(2)}, u32[]{:S(2)}) collective-permute-start(bf16[256,2432]{1,0:T(8,128)(2,1)S(1)} %get-tuple-element.106), channel_id=1, source_target_pairs={{0,32},{1,33},{2,34},{3,35},{4,36},{5,37},{6,38},{7,39},{8,40},{9,... | collective-permute-start | bytes 3735560 | tf_op jit(solution)/shard_map/ppermute | solution.py:41
  75.3 24.2 %copy-start.19 = (bf16[256,2304]{1,0:T(8,128)(2,1)}, bf16[256,2304]{1,0:T(8,128)(2,1)S(1)}, u32[]{:S(2)}) copy-start(bf16[256,2304]{1,0:T(8,128)(2,1)S(1)} %collective-permute-done.29.refs_9_) | copy-start | bytes 3538948
  75.3 7.2 %collective-permute-start.30 = (bf16[128,2304]{1,0:T(8,128)(2,1)S(1)}, bf16[128,2304]{1,0:T(8,128)(2,1)S(1)}, u32[]{:S(2)}, u32[]{:S(2)}) collective-permute-start(bf16[128,2304]{1,0:T(8,128)(2,1)S(1)} %slice.20), channel_id=1, source_target_pairs={{0,16},{1,17},{2,18},{3,19},{4,20},{5,21},{6,22},{7,23},{8,24},{9,... | collective-permute-start | bytes 1769480 | tf_op jit(solution)/shard_map/ppermute | solution.py:41
  78.8 20.6 %collective-permute-start.26 = (bf16[128,2432]{1,0:T(8,128)(2,1)S(1)}, bf16[128,2432]{1,0:T(8,128)(2,1)S(1)}, u32[]{:S(2)}, u32[]{:S(2)}) collective-permute-start(bf16[128,2432]{1,0:T(8,128)(2,1)S(1)} %slice.19), channel_id=1, source_target_pairs={{0,16},{1,17},{2,18},{3,19},{4,20},{5,21},{6,22},{7,23},{8,24},{9,... | collective-permute-start | bytes 1867784 | tf_op jit(solution)/shard_map/ppermute | solution.py:41
  79.3 20.1 %collective-permute-start.27 = (bf16[128,2432]{1,0:T(8,128)(2,1)S(1)}, bf16[128,2432]{1,0:T(8,128)(2,1)S(1)}, u32[]{:S(2)}, u32[]{:S(2)}) collective-permute-start(bf16[128,2432]{1,0:T(8,128)(2,1)S(1)} %get-tuple-element.115), channel_id=1, source_target_pairs={{0,8},{1,9},{2,10},{3,11},{4,12},{5,13},{6,14},{7,15},{8,0},{9,1},... | collective-permute-start | bytes 1867784 | tf_op jit(solution)/shard_map/ppermute | solution.py:41
  81.0 18.4 %copy-start.18 = (bf16[256,2432]{1,0:T(8,128)(2,1)}, bf16[256,2432]{1,0:T(8,128)(2,1)S(1)}, u32[]{:S(2)}) copy-start(bf16[256,2432]{1,0:T(8,128)(2,1)S(1)} %collective-permute-done.21.refs_1_) | copy-start | bytes 3735556
  81.1 18.3 %collective-permute-start.22 = (bf16[128,2432]{1,0:T(8,128)(2,1)S(1)}, bf16[128,2432]{1,0:T(8,128)(2,1)S(1)}, u32[]{:S(2)}, u32[]{:S(2)}) collective-permute-start(bf16[128,2432]{1,0:T(8,128)(2,1)S(1)} %slice.18), channel_id=1, source_target_pairs={{0,16},{1,17},{2,18},{3,19},{4,20},{5,21},{6,22},{7,23},{8,24},{9,... | collective-permute-start | bytes 1867784 | tf_op jit(solution)/shard_map/ppermute | solution.py:41
  81.3 18.1 %collective-permute-start.23 = (bf16[128,2432]{1,0:T(8,128)(2,1)S(1)}, bf16[128,2432]{1,0:T(8,128)(2,1)S(1)}, u32[]{:S(2)}, u32[]{:S(2)}) collective-permute-start(bf16[128,2432]{1,0:T(8,128)(2,1)S(1)} %get-tuple-element.108), channel_id=1, source_target_pairs={{0,64},{1,65},{2,66},{3,67},{4,68},{5,69},{6,70},{7,71},{8,72},{9,... | collective-permute-start | bytes 1867784 | tf_op jit(solution)/shard_map/ppermute | solution.py:41
  82.5 16.9 %collective-permute-start.31 = (bf16[128,2304]{1,0:T(8,128)(2,1)S(1)}, bf16[128,2304]{1,0:T(8,128)(2,1)S(1)}, u32[]{:S(2)}, u32[]{:S(2)}) collective-permute-start(bf16[128,2304]{1,0:T(8,128)(2,1)S(1)} %get-tuple-element.122), channel_id=1, source_target_pairs={{0,2},{1,3},{2,0},{3,1},{4,6},{5,7},{6,4},{7,5},{8,10},{9,11},{10,... | collective-permute-start | bytes 1769480 | tf_op jit(solution)/shard_map/ppermute | solution.py:41
  120.9 3.6 %collective-permute-start.40 = (bf16[128,2432]{1,0:T(8,128)(2,1)}, bf16[128,2432]{1,0:T(8,128)(2,1)S(1)}, u32[]{:S(2)}, u32[]{:S(2)}) collective-permute-start(bf16[128,2432]{1,0:T(8,128)(2,1)} %get-tuple-element.136), channel_id=1, source_target_pairs={{0,16},{1,17},{2,18},{3,19},{4,20},{5,21},{6,22},{7,23},{8,24},{9,... | collective-permute-start | bytes 1867784 | tf_op jit(solution)/shard_map/ppermute | solution.py:41
  121.2 6.5 %collective-permute-start.32 = (bf16[128,2432]{1,0:T(8,128)(2,1)}, bf16[128,2432]{1,0:T(8,128)(2,1)S(1)}, u32[]{:S(2)}, u32[]{:S(2)}) collective-permute-start(bf16[128,2432]{1,0:T(8,128)(2,1)} %get-tuple-element.125), channel_id=1, source_target_pairs={{0,16},{1,17},{2,18},{3,19},{4,20},{5,21},{6,22},{7,23},{8,24},{9,... | collective-permute-start | bytes 1867784 | tf_op jit(solution)/shard_map/ppermute | solution.py:41
  121.7 7.7 %collective-permute-start.48 = (bf16[128,2304]{1,0:T(8,128)(2,1)S(1)}, bf16[128,2304]{1,0:T(8,128)(2,1)S(1)}, u32[]{:S(2)}, u32[]{:S(2)}) collective-permute-start(bf16[128,2304]{1,0:T(8,128)(2,1)S(1)} %get-tuple-element.147), channel_id=1, source_target_pairs={{0,16},{1,17},{2,18},{3,19},{4,20},{5,21},{6,22},{7,23},{8,24},{9,... | collective-permute-start | bytes 1769480 | tf_op jit(solution)/shard_map/ppermute | solution.py:41
  121.8 18.6 %collective-permute-start.42 = (bf16[128,2432]{1,0:T(8,128)(2,1)}, bf16[128,2432]{1,0:T(8,128)(2,1)S(1)}, u32[]{:S(2)}, u32[]{:S(2)}) collective-permute-start(bf16[128,2432]{1,0:T(8,128)(2,1)} %get-tuple-element.137), channel_id=1, source_target_pairs={{0,8},{1,9},{2,10},{3,11},{4,12},{5,13},{6,14},{7,15},{8,0},{9,1},... | collective-permute-start | bytes 1867784 | tf_op jit(solution)/shard_map/ppermute | solution.py:41
  125.7 27.9 %collective-permute-start.41 = (bf16[256,2432]{1,0:T(8,128)(2,1)S(1)}, bf16[256,2432]{1,0:T(8,128)(2,1)S(1)}, u32[]{:S(2)}, u32[]{:S(2)}) collective-permute-start(bf16[256,2432]{1,0:T(8,128)(2,1)S(1)} %pad_maximum_fusion.1), channel_id=1, source_target_pairs={{0,12},{1,13},{2,14},{3,15},{4,0},{5,1},{6,2},{7,3},{8,4},{9,5},{1... | collective-permute-start | bytes 3735560 | tf_op jit(solution)/shard_map/ppermute | solution.py:41
  127.8 25.7 %copy-start.1 = (bf16[128,2432]{1,0:T(8,128)(2,1)S(1)}, bf16[128,2432]{1,0:T(8,128)(2,1)}, u32[]{:S(2)}) copy-start(bf16[128,2432]{1,0:T(8,128)(2,1)} %get-tuple-element.134.refs_0_) | copy-start | bytes 1867780
  127.8 26.3 %collective-permute-start.33 = (bf16[256,2432]{1,0:T(8,128)(2,1)S(1)}, bf16[256,2432]{1,0:T(8,128)(2,1)S(1)}, u32[]{:S(2)}, u32[]{:S(2)}) collective-permute-start(bf16[256,2432]{1,0:T(8,128)(2,1)S(1)} %pad_maximum_fusion), channel_id=1, source_target_pairs={{0,96},{1,97},{2,98},{3,99},{4,100},{5,101},{6,102},{7,103},{8,104... | collective-permute-start | bytes 3735560 | tf_op jit(solution)/shard_map/ppermute | solution.py:41
  129.5 28.6 %collective-permute-start.49 = (bf16[256,2304]{1,0:T(8,128)(2,1)S(1)}, bf16[256,2304]{1,0:T(8,128)(2,1)S(1)}, u32[]{:S(2)}, u32[]{:S(2)}) collective-permute-start(bf16[256,2304]{1,0:T(8,128)(2,1)S(1)} %pad_maximum_fusion.2), channel_id=1, source_target_pairs={{0,3},{1,0},{2,1},{3,2},{4,7},{5,4},{6,5},{7,6},{8,11},{9,8},{10,9... | collective-permute-start | bytes 3538952 | tf_op jit(solution)/shard_map/ppermute | solution.py:41
  131.4 22.8 %collective-permute-start.34 = (bf16[128,2432]{1,0:T(8,128)(2,1)S(1)}, bf16[128,2432]{1,0:T(8,128)(2,1)S(1)}, u32[]{:S(2)}, u32[]{:S(2)}) collective-permute-start(bf16[128,2432]{1,0:T(8,128)(2,1)S(1)} %copy-done.20), channel_id=1, source_target_pairs={{0,64},{1,65},{2,66},{3,67},{4,68},{5,69},{6,70},{7,71},{8,72},{9,... | collective-permute-start | bytes 1867784 | tf_op jit(solution)/shard_map/ppermute | solution.py:41
  140.4 17.7 %collective-permute-start.50 = (bf16[128,2304]{1,0:T(8,128)(2,1)S(1)}, bf16[128,2304]{1,0:T(8,128)(2,1)S(1)}, u32[]{:S(2)}, u32[]{:S(2)}) collective-permute-start(bf16[128,2304]{1,0:T(8,128)(2,1)S(1)} %copy-done.25), channel_id=1, source_target_pairs={{0,2},{1,3},{2,0},{3,1},{4,6},{5,7},{6,4},{7,5},{8,10},{9,11},{10,... | collective-permute-start | bytes 1769480 | tf_op jit(solution)/shard_map/ppermute | solution.py:41
  154.0 4.6 %collective-permute-start.43 = (bf16[256,2432]{1,0:T(8,128)(2,1)S(1)}, bf16[256,2432]{1,0:T(8,128)(2,1)S(1)}, u32[]{:S(2)}, u32[]{:S(2)}) collective-permute-start(bf16[256,2432]{1,0:T(8,128)(2,1)S(1)} %other1.1), channel_id=1, source_target_pairs={{0,16},{1,17},{2,18},{3,19},{4,20},{5,21},{6,22},{7,23},{8,24},{9,... | collective-permute-start | bytes 3735560 | tf_op jit(solution)/shard_map/ppermute | solution.py:41
  155.1 8.0 %collective-permute-start.35 = (bf16[256,2432]{1,0:T(8,128)(2,1)S(1)}, bf16[256,2432]{1,0:T(8,128)(2,1)S(1)}, u32[]{:S(2)}, u32[]{:S(2)}) collective-permute-start(bf16[256,2432]{1,0:T(8,128)(2,1)S(1)} %other0.1), channel_id=1, source_target_pairs={{0,16},{1,17},{2,18},{3,19},{4,20},{5,21},{6,22},{7,23},{8,24},{9,... | collective-permute-start | bytes 3735560 | tf_op jit(solution)/shard_map/ppermute | solution.py:41
  158.6 6.9 %collective-permute-start.51 = (bf16[256,2304]{1,0:T(8,128)(2,1)S(1)}, bf16[256,2304]{1,0:T(8,128)(2,1)S(1)}, u32[]{:S(2)}, u32[]{:S(2)}) collective-permute-start(bf16[256,2304]{1,0:T(8,128)(2,1)S(1)} %other2.1), channel_id=1, source_target_pairs={{0,16},{1,17},{2,18},{3,19},{4,20},{5,21},{6,22},{7,23},{8,24},{9,... | collective-permute-start | bytes 3538952 | tf_op jit(solution)/shard_map/ppermute | solution.py:41
  159.2 12.0 %collective-permute-start.44 = (bf16[128,2432]{1,0:T(8,128)(2,1)S(1)}, bf16[128,2432]{1,0:T(8,128)(2,1)S(1)}, u32[]{:S(2)}, u32[]{:S(2)}) collective-permute-start(bf16[128,2432]{1,0:T(8,128)(2,1)S(1)} %get-tuple-element.140), channel_id=1, source_target_pairs={{0,96},{1,97},{2,98},{3,99},{4,100},{5,101},{6,102},{7,103},{8,104... | collective-permute-start | bytes 1867784 | tf_op jit(solution)/shard_map/ppermute | solution.py:41
  163.6 10.3 %collective-permute-start.36 = (bf16[128,2432]{1,0:T(8,128)(2,1)S(1)}, bf16[128,2432]{1,0:T(8,128)(2,1)S(1)}, u32[]{:S(2)}, u32[]{:S(2)}) collective-permute-start(bf16[128,2432]{1,0:T(8,128)(2,1)S(1)} %get-tuple-element.129), channel_id=1, source_target_pairs={{0,3},{1,0},{2,1},{3,2},{4,7},{5,4},{6,5},{7,6},{8,11},{9,8},{10,9... | collective-permute-start | bytes 1867784 | tf_op jit(solution)/shard_map/ppermute | solution.py:41
  165.9 11.4 %collective-permute-start.52 = (bf16[128,2304]{1,0:T(8,128)(2,1)S(1)}, bf16[128,2304]{1,0:T(8,128)(2,1)S(1)}, u32[]{:S(2)}, u32[]{:S(2)}) collective-permute-start(bf16[128,2304]{1,0:T(8,128)(2,1)S(1)} %get-tuple-element.151), channel_id=1, source_target_pairs={{0,12},{1,13},{2,14},{3,15},{4,0},{5,1},{6,2},{7,3},{8,4},{9,5},{1... | collective-permute-start | bytes 1769480 | tf_op jit(solution)/shard_map/ppermute | solution.py:41
  171.2 6.4 %collective-permute-start.46 = (bf16[64,2432]{1,0:T(8,128)(2,1)S(1)}, bf16[64,2432]{1,0:T(8,128)(2,1)S(1)}, u32[]{:S(2)}, u32[]{:S(2)}) collective-permute-start(bf16[64,2432]{1,0:T(8,128)(2,1)S(1)} %slice.22), channel_id=1, source_target_pairs={{0,16},{1,17},{2,18},{3,19},{4,20},{5,21},{6,22},{7,23},{8,24},{9,... | collective-permute-start | bytes 933896 | tf_op jit(solution)/shard_map/ppermute | solution.py:41
  171.3 11.3 %collective-permute-start.45 = (bf16[64,2432]{1,0:T(8,128)(2,1)S(1)}, bf16[64,2432]{1,0:T(8,128)(2,1)S(1)}, u32[]{:S(2)}, u32[]{:S(2)}) collective-permute-start(bf16[64,2432]{1,0:T(8,128)(2,1)S(1)} %get-tuple-element.142), channel_id=1, source_target_pairs={{0,64},{1,65},{2,66},{3,67},{4,68},{5,69},{6,70},{7,71},{8,72},{9,... | collective-permute-start | bytes 933896 | tf_op jit(solution)/shard_map/ppermute | solution.py:41
  173.9 10.9 %collective-permute-start.38 = (bf16[64,2432]{1,0:T(8,128)(2,1)S(1)}, bf16[64,2432]{1,0:T(8,128)(2,1)S(1)}, u32[]{:S(2)}, u32[]{:S(2)}) collective-permute-start(bf16[64,2432]{1,0:T(8,128)(2,1)S(1)} %slice.21), channel_id=1, source_target_pairs={{0,16},{1,17},{2,18},{3,19},{4,20},{5,21},{6,22},{7,23},{8,24},{9,... | collective-permute-start | bytes 933896 | tf_op jit(solution)/shard_map/ppermute | solution.py:41
  174.0 11.3 %collective-permute-start.37 = (bf16[64,2432]{1,0:T(8,128)(2,1)S(1)}, bf16[64,2432]{1,0:T(8,128)(2,1)S(1)}, u32[]{:S(2)}, u32[]{:S(2)}) collective-permute-start(bf16[64,2432]{1,0:T(8,128)(2,1)S(1)} %get-tuple-element.131), channel_id=1, source_target_pairs={{0,2},{1,3},{2,0},{3,1},{4,6},{5,7},{6,4},{7,5},{8,10},{9,11},{10,... | collective-permute-start | bytes 933896 | tf_op jit(solution)/shard_map/ppermute | solution.py:41
  177.4 8.6 %collective-permute-start.54 = (bf16[64,2304]{1,0:T(8,128)(2,1)S(1)}, bf16[64,2304]{1,0:T(8,128)(2,1)S(1)}, u32[]{:S(2)}, u32[]{:S(2)}) collective-permute-start(bf16[64,2304]{1,0:T(8,128)(2,1)S(1)} %slice.23), channel_id=1, source_target_pairs={{0,16},{1,17},{2,18},{3,19},{4,20},{5,21},{6,22},{7,23},{8,24},{9,... | collective-permute-start | bytes 884744 | tf_op jit(solution)/shard_map/ppermute | solution.py:41
  177.6 11.3 %collective-permute-start.53 = (bf16[64,2304]{1,0:T(8,128)(2,1)S(1)}, bf16[64,2304]{1,0:T(8,128)(2,1)S(1)}, u32[]{:S(2)}, u32[]{:S(2)}) collective-permute-start(bf16[64,2304]{1,0:T(8,128)(2,1)S(1)} %get-tuple-element.153), channel_id=1, source_target_pairs={{0,8},{1,9},{2,10},{3,11},{4,12},{5,13},{6,14},{7,15},{8,0},{9,1},... | collective-permute-start | bytes 884744 | tf_op jit(solution)/shard_map/ppermute | solution.py:41
  182.7 11.6 %collective-permute-start.47 = (bf16[32,2432]{1,0:T(8,128)(2,1)S(1)}, bf16[32,2432]{1,0:T(8,128)(2,1)S(1)}, u32[]{:S(2)}, u32[]{:S(2)}) collective-permute-start(bf16[32,2432]{1,0:T(8,128)(2,1)S(1)} %get-tuple-element.143), channel_id=1, source_target_pairs={{0,3},{1,0},{2,1},{3,2},{4,7},{5,4},{6,5},{7,6},{8,11},{9,8},{10,9... | collective-permute-start | bytes 466952 | tf_op jit(solution)/shard_map/ppermute | solution.py:41
  185.4 8.9 %collective-permute-start.39 = (bf16[32,2432]{1,0:T(8,128)(2,1)S(1)}, bf16[32,2432]{1,0:T(8,128)(2,1)S(1)}, u32[]{:S(2)}, u32[]{:S(2)}) collective-permute-start(bf16[32,2432]{1,0:T(8,128)(2,1)S(1)} %get-tuple-element.132), channel_id=1, source_target_pairs={{0,12},{1,13},{2,14},{3,15},{4,0},{5,1},{6,2},{7,3},{8,4},{9,5},{1... | collective-permute-start | bytes 466952 | tf_op jit(solution)/shard_map/ppermute | solution.py:41
  189.1 5.2 %collective-permute-start.55 = (bf16[32,2304]{1,0:T(8,128)(2,1)S(1)}, bf16[32,2304]{1,0:T(8,128)(2,1)S(1)}, u32[]{:S(2)}, u32[]{:S(2)}) collective-permute-start(bf16[32,2304]{1,0:T(8,128)(2,1)S(1)} %get-tuple-element.154), channel_id=1, source_target_pairs={{0,96},{1,97},{2,98},{3,99},{4,100},{5,101},{6,102},{7,103},{8,104... | collective-permute-start | bytes 442376 | tf_op jit(solution)/shard_map/ppermute | solution.py:41
  194.3 8.4 %collective-permute-start.56 = (bf16[16,7168]{1,0:T(8,128)(2,1)S(1)}, bf16[16,7168]{1,0:T(8,128)(2,1)S(1)}, u32[]{:S(2)}, u32[]{:S(2)}) collective-permute-start(bf16[16,7168]{1,0:T(8,128)(2,1)S(1)} %cross.1), channel_id=1, source_target_pairs={{0,16},{1,17},{2,18},{3,19},{4,20},{5,21},{6,22},{7,23},{8,24},{9,... | collective-permute-start | bytes 688136 | tf_op jit(solution)/shard_map/ppermute | solution.py:41
  194.4 8.3 %collective-permute-start.58 = (bf16[16,2432]{1,0:T(8,128)(2,1)S(1)}, bf16[16,2432]{1,0:T(8,128)(2,1)S(1)}, u32[]{:S(2)}, u32[]{:S(2)}) collective-permute-start(bf16[16,2432]{1,0:T(8,128)(2,1)S(1)} %get-tuple-element.158), channel_id=1, source_target_pairs={{0,2},{1,3},{2,0},{3,1},{4,6},{5,7},{6,4},{7,5},{8,10},{9,11},{10,... | collective-permute-start | bytes 233480 | tf_op jit(solution)/shard_map/ppermute | solution.py:41
  195.2 7.6 %collective-permute-start.57 = (bf16[16,2432]{1,0:T(8,128)(2,1)S(1)}, bf16[16,2432]{1,0:T(8,128)(2,1)S(1)}, u32[]{:S(2)}, u32[]{:S(2)}) collective-permute-start(bf16[16,2432]{1,0:T(8,128)(2,1)S(1)} %get-tuple-element.156), channel_id=1, source_target_pairs={{0,8},{1,9},{2,10},{3,11},{4,12},{5,13},{6,14},{7,15},{8,0},{9,1},... | collective-permute-start | bytes 233480 | tf_op jit(solution)/shard_map/ppermute | solution.py:41
  196.9 5.9 %collective-permute-start.59 = (bf16[16,2304]{1,0:T(8,128)(2,1)S(1)}, bf16[16,2304]{1,0:T(8,128)(2,1)S(1)}, u32[]{:S(2)}, u32[]{:S(2)}) collective-permute-start(bf16[16,2304]{1,0:T(8,128)(2,1)S(1)} %get-tuple-element.160), channel_id=1, source_target_pairs={{0,64},{1,65},{2,66},{3,67},{4,68},{5,69},{6,70},{7,71},{8,72},{9,... | collective-permute-start | bytes 221192 | tf_op jit(solution)/shard_map/ppermute | solution.py:41
  (24 other events, 73.8 us)
where the time goes:
time: 204 us
  waiting for transfers between devices  92.3 us (45%)
  starting transfers between devices  67.9 us (33%)
  Pallas kernels  30.3 us (15%)
  local copies, waits for them, and re-layouts  8.88 us (4%)
  other arithmetic  3.28 us (2%)
    ppermute x60, waiting for transfers between devices, from_offset(): return lax.ppermute(value, AXES, pairs)  92.3 us
    ppermute x60, starting transfers between devices, from_offset(): return lax.ppermute(value, AXES, pairs)  67.9 us
    pallas_call x1, Pallas kernels, expert_halves(): pl.pallas_call(functools.partial(expert_kernel, starts, sizes), out_shape...  19.8 us
    unnamed x61, local copies, waits for them, and re-layouts  8.58 us
    pallas_call x3, Pallas kernels, pack(): pl.pallas_call(functools.partial(pack_kernel, size, color), out_shape=[ja...  6.36 us
  transfers between devices with their start and end apart: 60, of which 25 were waited for; matrix products, arithmetic and copies ran while one was open for 2% of the time, Pallas kernels for 5%

commit v1 on v0

--- a/solution.py
+++ b/solution.py
@@ -11,8 +11,8 @@
 ORDERS = (("x", "y", "z"), ("y", "z", "x"), ("z", "x", "y"))
 RING = 4
 META = 128
-WIDE_PARAMS = pltpu.CompilerParams(vmem_limit_bytes=52 * 1024 * 1024)
-PARAMS = pltpu.CompilerParams(vmem_limit_bytes=24 * 1024 * 1024)
+WIDE_PARAMS = pltpu.CompilerParams(vmem_limit_bytes=40 * 1024 * 1024)
+PARAMS = pltpu.CompilerParams(vmem_limit_bytes=14 * 1024 * 1024)
 BF16, F32 = jnp.bfloat16, jnp.float32
 
 
@@ -270,7 +270,7 @@
     results = pl.pallas_call(
         functools.partial(expert_kernel, starts, sizes),
         out_shape=[jax.ShapeDtypeStruct((128, size), BF16) for size in sizes for _ in range(4)],
-        in_specs=[everywhere] * 15,
+        in_specs=[everywhere] * 12 + [pl.BlockSpec(memory_space=pltpu.HBM)] * 3,
         out_specs=[everywhere] * 12,
         scratch_shapes=[pltpu.VMEM((512, size), BF16) for size in sizes]
         + [
@@ -286,7 +286,10 @@
         compiler_params=WIDE_PARAMS,
         cost_estimate=cost(6 * 512 * gate.size, 6 * gate.size + 4 * 512 * gate.shape[0]),
         name="experts",
-    )(*[ref for mine in rows for ref in mine], gate, up, down)
+    )(
+        *[ref for mine in rows for ref in mine],
+        *[pltpu.with_memory_space_constraint(weight, pltpu.HBM) for weight in (gate, up, down)],
+    )
     return [results[4 * k : 4 * k + 4] for k in range(3)]
 
 

time: 204 us -> 201 us (0.985)
  local copies, waits for them, and re-layouts: 8.88 us -> 5.9 us
    unnamed x61 -> x31, local copies, waits for them, and re-layouts: 8.58 us -> 5.6 us
  transfers between devices with their start and end apart: 60 -> 60, of which waited for: 25 -> 25; matrix products, arithmetic and copies ran while one was open for 2% -> 1% of each run, Pallas kernels for 5% -> 5%
where the time goes in v1:
time: 201 us; the launch traced here: 200 us
  waiting for transfers between devices  91.9 us (46%)
  starting transfers between devices  69 us (34%)
  Pallas kernels  30.8 us (15%)
  local copies, waits for them, and re-layouts  5.9 us (3%)
  other arithmetic  2.12 us (1%)
    ppermute x60, waiting for transfers between devices, from_offset(): return lax.ppermute(value, AXES, pairs)  91.9 us
    ppermute x60, starting transfers between devices, from_offset(): return lax.ppermute(value, AXES, pairs)  69 us
    pallas_call x1, Pallas kernels, expert_halves(): pl.pallas_call(functools.partial(expert_kernel, starts, sizes), out_shape...  20.2 us
    pallas_call x3, Pallas kernels, pack(): pl.pallas_call(functools.partial(pack_kernel, size, color), out_shape=[ja...  6.36 us
    unnamed x31, local copies, waits for them, and re-layouts  5.6 us
  transfers between devices with their start and end apart: 60, of which 25 were waited for; matrix products, arithmetic and copies ran while one was open for 1% of the time, Pallas kernels for 5%

profile of v1, /device:TPU:0, one launch (start us, length us, event | category | flops | bytes accessed | tf_op | source)
XLA Modules:
  0.0 200.5 jit_solution(11569516931827193881)
XLA Ops:
  0.8 0.8 maximum_maximum_fusion.info_ref
  2.2 0.8 collective-permute-done.1.info2_ref
  3.0 0.9 copy-done.10
  4.0 4.0 %collective-permute-start.7 = (bf16[16,2432]{1,0:T(8,128)(2,1)S(1)}, bf16[16,2432]{1,0:T(8,128)(2,1)S(1)}, u32[]{:S(2)}, u32[]{:S(2)}) collective-permute-start(bf16[16,2432]{1,0:T(8,128)(2,1)S(1)} %get-tuple-element.88), channel_id=1, source_target_pairs={{0,64},{1,65},{2,66},{3,67},{4,68},{5,69},{6,70},{7,71},{8,72},{9,... | collective-permute-start | bytes 233480 | tf_op jit(solution)/shard_map/ppermute | solution.py:41
  8.0 3.0 %collective-permute-start.5 = (bf16[16,2560]{1,0:T(8,128)(2,1)S(1)}, bf16[16,2560]{1,0:T(8,128)(2,1)S(1)}, u32[]{:S(2)}, u32[]{:S(2)}) collective-permute-start(bf16[16,2560]{1,0:T(8,128)(2,1)S(1)} %get-tuple-element.83), channel_id=1, source_target_pairs={{0,8},{1,9},{2,10},{3,11},{4,12},{5,13},{6,14},{7,15},{8,0},{9,1},... | collective-permute-start | bytes 245768 | tf_op jit(solution)/shard_map/ppermute | solution.py:41
  11.0 3.2 %collective-permute-start.6 = (bf16[16,2560]{1,0:T(8,128)(2,1)S(1)}, bf16[16,2560]{1,0:T(8,128)(2,1)S(1)}, u32[]{:S(2)}, u32[]{:S(2)}) collective-permute-start(bf16[16,2560]{1,0:T(8,128)(2,1)S(1)} %get-tuple-element.87), channel_id=1, source_target_pairs={{0,2},{1,3},{2,0},{3,1},{4,6},{5,7},{6,4},{7,5},{8,10},{9,11},{10,... | collective-permute-start | bytes 245768 | tf_op jit(solution)/shard_map/ppermute | solution.py:41
  14.3 1.1 collective-permute-start.4
  17.0 3.8 %collective-permute-done.4 = bf16[32,2432]{1,0:T(8,128)(2,1)S(1)} collective-permute-done((bf16[32,2432]{1,0:T(8,128)(2,1)S(1)}, bf16[32,2432]{1,0:T(8,128)(2,1)S(1)}, u32[]{:S(2)}, u32[]{:S(2)}) %collective-permute-start.4) | collective-permute-done | bytes 155680 | tf_op jit(solution)/shard_map/ppermute | solution.py:41
  20.8 1.1 collective-permute-done.2
  22.5 2.1 %collective-permute-start.13 = (bf16[64,2432]{1,0:T(8,128)(2,1)S(1)}, bf16[64,2432]{1,0:T(8,128)(2,1)S(1)}, u32[]{:S(2)}, u32[]{:S(2)}) collective-permute-start(bf16[64,2432]{1,0:T(8,128)(2,1)S(1)} %constant_dynamic-update-slice_fusion.6), channel_id=1, source_target_pairs={{0,8},{1,9},{2,10},{3,11},{4,12},{5,13},{6,14},{7,15},{8,0},{9,1},... | collective-permute-start | bytes 933896 | tf_op jit(solution)/shard_map/ppermute | solution.py:41
  24.6 1.2 collective-permute-start.12
  26.6 0.8 collective-permute-done.9
  28.0 3.0 %collective-permute-done.13.refs_2_ = bf16[64,2432]{1,0:T(8,128)(2,1)S(1)} collective-permute-done((bf16[64,2432]{1,0:T(8,128)(2,1)S(1)}, bf16[64,2432]{1,0:T(8,128)(2,1)S(1)}, u32[]{:S(2)}, u32[]{:S(2)}) %collective-permute-start.13) | collective-permute-done | bytes 311328 | tf_op jit(solution)/shard_map/ppermute | solution.py:41
  31.0 5.3 %collective-permute-done.12.refs_2_ = bf16[64,2560]{1,0:T(8,128)(2,1)S(1)} collective-permute-done((bf16[64,2560]{1,0:T(8,128)(2,1)S(1)}, bf16[64,2560]{1,0:T(8,128)(2,1)S(1)}, u32[]{:S(2)}, u32[]{:S(2)}) %collective-permute-start.12) | collective-permute-done | bytes 327712 | tf_op jit(solution)/shard_map/ppermute | solution.py:41
  36.3 1.3 collective-permute-done.11.refs_2_
  37.6 1.9 collective-permute-start.15
  39.5 1.5 collective-permute-start.16
  41.0 0.7 copy-done
  41.8 0.7 copy-done.8
  43.0 0.7 copy-done.2
  43.7 0.7 copy-done.4
  45.2 5.9 %collective-permute-done.16.refs_1_ = bf16[128,2432]{1,0:T(8,128)(2,1)} collective-permute-done((bf16[128,2432]{1,0:T(8,128)(2,1)S(1)}, bf16[128,2432]{1,0:T(8,128)(2,1)}, u32[]{:S(2)}, u32[]{:S(2)}) %collective-permute-start.16) | collective-permute-done | bytes 622624 | tf_op jit(solution)/shard_map/ppermute | solution.py:41
  52.2 1.3 collective-permute-done.28.refs_3_
  53.5 1.0 copy-done.9
  54.5 2.6 %pack2.1 = (bf16[128,2304]{1,0:T(8,128)(2,1)S(1)}, bf16[256,2304]{1,0:T(8,128)(2,1)S(1)}, bf16[128,2304]{1,0:T(8,128)(2,1)S(1)}, bf16[512,128]{1,0:T(8,128)(2,1)S(1)}) custom-call(s32[3,4]{1,0:T(4,128)S(1)} %pad_add_fusion.experts_ref, bf16[128,2432]{1,0:T(8,128)(2,1)S(1)} %pad_maximum_fusion.5.refs_0_, bf16[128,2432]{1,0:T(8,128)(2,1)} %collective-permute-done.16.refs_1_, ...), custom_call_target="tpu_custom_call" | custom-call | flops 150994944 | bytes 4718592 | tf_op jit(solution)/shard_map/pack2/pallas_call | solution.py:146
  57.7 1.9 pack1.1
  60.2 1.9 pack0.1
  62.1 0.9 collective-permute-start.21
  63.0 11.5 %collective-permute-done.29.refs_9_ = bf16[256,2304]{1,0:T(8,128)(2,1)S(1)} collective-permute-done((bf16[256,2304]{1,0:T(8,128)(2,1)S(1)}, bf16[256,2304]{1,0:T(8,128)(2,1)S(1)}, u32[]{:S(2)}, u32[]{:S(2)}) %collective-permute-start.29) | collective-permute-done | bytes 1179680 | tf_op jit(solution)/shard_map/ppermute | solution.py:41
  74.7 3.3 %collective-permute-done.25.refs_5_ = bf16[256,2432]{1,0:T(8,128)(2,1)S(1)} collective-permute-done((bf16[256,2432]{1,0:T(8,128)(2,1)S(1)}, bf16[256,2432]{1,0:T(8,128)(2,1)S(1)}, u32[]{:S(2)}, u32[]{:S(2)}) %collective-permute-start.25) | collective-permute-done | bytes 1245216 | tf_op jit(solution)/shard_map/ppermute | solution.py:41
  78.9 1.4 collective-permute-done.21.refs_1_
  80.5 1.2 collective-permute-start.23
  81.7 3.0 %collective-permute-start.31 = (bf16[128,2304]{1,0:T(8,128)(2,1)S(1)}, bf16[128,2304]{1,0:T(8,128)(2,1)S(1)}, u32[]{:S(2)}, u32[]{:S(2)}) collective-permute-start(bf16[128,2304]{1,0:T(8,128)(2,1)S(1)} %get-tuple-element.122), channel_id=1, source_target_pairs={{0,2},{1,3},{2,0},{3,1},{4,6},{5,7},{6,4},{7,5},{8,10},{9,11},{10,... | collective-permute-start | bytes 1769480 | tf_op jit(solution)/shard_map/ppermute | solution.py:41
  84.7 13.9 %collective-permute-done.31.refs_11_ = bf16[128,2304]{1,0:T(8,128)(2,1)S(1)} collective-permute-done((bf16[128,2304]{1,0:T(8,128)(2,1)S(1)}, bf16[128,2304]{1,0:T(8,128)(2,1)S(1)}, u32[]{:S(2)}, u32[]{:S(2)}) %collective-permute-start.31) | collective-permute-done | bytes 589856 | tf_op jit(solution)/shard_map/ppermute | solution.py:41
  98.6 20.2 %experts.1 = (bf16[128,2432]{1,0:T(8,128)(2,1)S(1)}, bf16[128,2432]{1,0:T(8,128)(2,1)S(1)}, bf16[128,2432]{1,0:T(8,128)(2,1)S(1)}, bf16[128,2432]{1,0:T(8,128)(2...) custom-call(bf16[128,2432]{1,0:T(8,128)(2,1)S(1)} %get-tuple-element, ...), custom_call_target="tpu_custom_call" | custom-call | flops 11274289152 | bytes 36700160 | tf_op jit(solution)/shard_map/experts/pallas_call | solution.py:270
  119.7 2.7 %collective-permute-start.42 = (bf16[128,2432]{1,0:T(8,128)(2,1)S(1)}, bf16[128,2432]{1,0:T(8,128)(2,1)S(1)}, u32[]{:S(2)}, u32[]{:S(2)}) collective-permute-start(bf16[128,2432]{1,0:T(8,128)(2,1)S(1)} %get-tuple-element.137), channel_id=1, source_target_pairs={{0,8},{1,9},{2,10},{3,11},{4,12},{5,13},{6,14},{7,15},{8,0},{9,1},... | collective-permute-start | bytes 1867784 | tf_op jit(solution)/shard_map/ppermute | solution.py:41
  122.5 1.8 collective-permute-start.41
  124.4 1.8 collective-permute-start.33
  126.3 1.7 collective-permute-start.49
  128.0 1.7 collective-permute-start.34
  129.7 8.5 %collective-permute-done.42.refs_2_ = bf16[128,2432]{1,0:T(8,128)(2,1)S(1)} collective-permute-done((bf16[128,2432]{1,0:T(8,128)(2,1)S(1)}, bf16[128,2432]{1,0:T(8,128)(2,1)S(1)}, u32[]{:S(2)}, u32[]{:S(2)}) %collective-permute-start.42) | collective-permute-done | bytes 622624 | tf_op jit(solution)/shard_map/ppermute | solution.py:41
  138.1 3.9 %collective-permute-start.50 = (bf16[128,2304]{1,0:T(8,128)(2,1)S(1)}, bf16[128,2304]{1,0:T(8,128)(2,1)S(1)}, u32[]{:S(2)}, u32[]{:S(2)}) collective-permute-start(bf16[128,2304]{1,0:T(8,128)(2,1)S(1)} %get-tuple-element.148), channel_id=1, source_target_pairs={{0,2},{1,3},{2,0},{3,1},{4,6},{5,7},{6,4},{7,5},{8,10},{9,11},{10,... | collective-permute-start | bytes 1769480 | tf_op jit(solution)/shard_map/ppermute | solution.py:41
  142.0 9.3 %collective-permute-done.41.refs_1_ = bf16[256,2432]{1,0:T(8,128)(2,1)S(1)} collective-permute-done((bf16[256,2432]{1,0:T(8,128)(2,1)S(1)}, bf16[256,2432]{1,0:T(8,128)(2,1)S(1)}, u32[]{:S(2)}, u32[]{:S(2)}) %collective-permute-start.41) | collective-permute-done | bytes 1245216 | tf_op jit(solution)/shard_map/ppermute | solution.py:41
  152.4 2.8 %collective-permute-start.35 = (bf16[256,2432]{1,0:T(8,128)(2,1)S(1)}, bf16[256,2432]{1,0:T(8,128)(2,1)S(1)}, u32[]{:S(2)}, u32[]{:S(2)}) collective-permute-start(bf16[256,2432]{1,0:T(8,128)(2,1)S(1)} %other0.1), channel_id=1, source_target_pairs={{0,16},{1,17},{2,18},{3,19},{4,20},{5,21},{6,22},{7,23},{8,24},{9,... | collective-permute-start | bytes 3735560 | tf_op jit(solution)/shard_map/ppermute | solution.py:41
  156.3 3.6 %collective-permute-start.44 = (bf16[128,2432]{1,0:T(8,128)(2,1)S(1)}, bf16[128,2432]{1,0:T(8,128)(2,1)S(1)}, u32[]{:S(2)}, u32[]{:S(2)}) collective-permute-start(bf16[128,2432]{1,0:T(8,128)(2,1)S(1)} %get-tuple-element.140), channel_id=1, source_target_pairs={{0,96},{1,97},{2,98},{3,99},{4,100},{5,101},{6,102},{7,103},{8,104... | collective-permute-start | bytes 1867784 | tf_op jit(solution)/shard_map/ppermute | solution.py:41
  160.4 2.2 %collective-permute-start.36 = (bf16[128,2432]{1,0:T(8,128)(2,1)S(1)}, bf16[128,2432]{1,0:T(8,128)(2,1)S(1)}, u32[]{:S(2)}, u32[]{:S(2)}) collective-permute-start(bf16[128,2432]{1,0:T(8,128)(2,1)S(1)} %get-tuple-element.129), channel_id=1, source_target_pairs={{0,3},{1,0},{2,1},{3,2},{4,7},{5,4},{6,5},{7,6},{8,11},{9,8},{10,9... | collective-permute-start | bytes 1867784 | tf_op jit(solution)/shard_map/ppermute | solution.py:41
  163.1 0.8 collective-permute-start.52
  163.9 3.9 %collective-permute-done.44.near_ref = bf16[128,2432]{1,0:T(8,128)(2,1)S(1)} collective-permute-done((bf16[128,2432]{1,0:T(8,128)(2,1)S(1)}, bf16[128,2432]{1,0:T(8,128)(2,1)S(1)}, u32[]{:S(2)}, u32[]{:S(2)}) %collective-permute-start.44) | collective-permute-done | bytes 622624 | tf_op jit(solution)/shard_map/ppermute | solution.py:41
  167.9 1.9 collective-permute-start.45
  169.7 0.9 collective-permute-done.36.near_ref
  170.8 3.7 %collective-permute-start.37 = (bf16[64,2432]{1,0:T(8,128)(2,1)S(1)}, bf16[64,2432]{1,0:T(8,128)(2,1)S(1)}, u32[]{:S(2)}, u32[]{:S(2)}) collective-permute-start(bf16[64,2432]{1,0:T(8,128)(2,1)S(1)} %get-tuple-element.131), channel_id=1, source_target_pairs={{0,2},{1,3},{2,0},{3,1},{4,6},{5,7},{6,4},{7,5},{8,10},{9,11},{10,... | collective-permute-start | bytes 933896 | tf_op jit(solution)/shard_map/ppermute | solution.py:41
  174.7 1.5 collective-permute-start.53
  176.2 2.9 %collective-permute-done.45.far_ref = bf16[64,2432]{1,0:T(8,128)(2,1)S(1)} collective-permute-done((bf16[64,2432]{1,0:T(8,128)(2,1)S(1)}, bf16[64,2432]{1,0:T(8,128)(2,1)S(1)}, u32[]{:S(2)}, u32[]{:S(2)}) %collective-permute-start.45) | collective-permute-done | bytes 311328 | tf_op jit(solution)/shard_map/ppermute | solution.py:41
  179.3 2.2 %collective-permute-start.47 = (bf16[32,2432]{1,0:T(8,128)(2,1)S(1)}, bf16[32,2432]{1,0:T(8,128)(2,1)S(1)}, u32[]{:S(2)}, u32[]{:S(2)}) collective-permute-start(bf16[32,2432]{1,0:T(8,128)(2,1)S(1)} %get-tuple-element.143), channel_id=1, source_target_pairs={{0,3},{1,0},{2,1},{3,2},{4,7},{5,4},{6,5},{7,6},{8,11},{9,8},{10,9... | collective-permute-start | bytes 466952 | tf_op jit(solution)/shard_map/ppermute | solution.py:41
  181.5 1.0 collective-permute-done.37.far_ref
  182.6 0.8 collective-permute-start.39
  183.4 2.6 %collective-permute-done.53.far_ref = bf16[64,2304]{1,0:T(8,128)(2,1)S(1)} collective-permute-done((bf16[64,2304]{1,0:T(8,128)(2,1)S(1)}, bf16[64,2304]{1,0:T(8,128)(2,1)S(1)}, u32[]{:S(2)}, u32[]{:S(2)}) %collective-permute-start.53) | collective-permute-done | bytes 294944 | tf_op jit(solution)/shard_map/ppermute | solution.py:41
  186.1 1.8 collective-permute-start.55
  187.9 3.5 %collective-permute-done.55.refs_2_.refs_7_ = bf16[32,2304]{1,0:T(8,128)(2,1)S(1)} collective-permute-done((bf16[32,2304]{1,0:T(8,128)(2,1)S(1)}, bf16[32,2304]{1,0:T(8,128)(2,1)S(1)}, u32[]{:S(2)}, u32[]{:S(2)}) %collective-permute-start.55) | collective-permute-done | bytes 147488 | tf_op jit(solution)/shard_map/ppermute | solution.py:41
  191.5 1.3 collective-permute-start.58
  192.7 1.0 collective-permute-start.57
  193.8 1.4 collective-permute-start.59
  195.2 4.5 %collective-permute-done.59.refs_8_ = bf16[16,2304]{1,0:T(8,128)(2,1)S(1)} collective-permute-done((bf16[16,2304]{1,0:T(8,128)(2,1)S(1)}, bf16[16,2304]{1,0:T(8,128)(2,1)S(1)}, u32[]{:S(2)}, u32[]{:S(2)}) %collective-permute-start.59) | collective-permute-done | bytes 73760 | tf_op jit(solution)/shard_map/ppermute | solution.py:41
  199.7 0.8 finish.1
  (125 shorter events, 14.6 us)
Async XLA Ops:
  0.0 3.0 %collective-permute-start = (bf16[16,7168]{1,0:T(8,128)(2,1)}, bf16[16,7168]{1,0:T(8,128)(2,1)S(1)}, u32[]{:S(2)}, u32[]{:S(2)}) collective-permute-start(bf16[16,7168]{1,0:T(8,128)(2,1)} %bitcast.26), channel_id=1, source_target_pairs={{0,16},{1,17},{2,18},{3,19},{4,20},{5,21},{6,22},{7,23},{8,24},{9,... | collective-permute-start | bytes 688136 | tf_op jit(solution)/shard_map/ppermute | solution.py:41
  1.6 1.4 collective-permute-start.1
  4.0 12.0 %collective-permute-start.7 = (bf16[16,2432]{1,0:T(8,128)(2,1)S(1)}, bf16[16,2432]{1,0:T(8,128)(2,1)S(1)}, u32[]{:S(2)}, u32[]{:S(2)}) collective-permute-start(bf16[16,2432]{1,0:T(8,128)(2,1)S(1)} %get-tuple-element.88), channel_id=1, source_target_pairs={{0,64},{1,65},{2,66},{3,67},{4,68},{5,69},{6,70},{7,71},{8,72},{9,... | collective-permute-start | bytes 233480 | tf_op jit(solution)/shard_map/ppermute | solution.py:41
  8.0 8.6 %collective-permute-start.5 = (bf16[16,2560]{1,0:T(8,128)(2,1)S(1)}, bf16[16,2560]{1,0:T(8,128)(2,1)S(1)}, u32[]{:S(2)}, u32[]{:S(2)}) collective-permute-start(bf16[16,2560]{1,0:T(8,128)(2,1)S(1)} %get-tuple-element.83), channel_id=1, source_target_pairs={{0,8},{1,9},{2,10},{3,11},{4,12},{5,13},{6,14},{7,15},{8,0},{9,1},... | collective-permute-start | bytes 245768 | tf_op jit(solution)/shard_map/ppermute | solution.py:41
  11.0 5.9 %collective-permute-start.6 = (bf16[16,2560]{1,0:T(8,128)(2,1)S(1)}, bf16[16,2560]{1,0:T(8,128)(2,1)S(1)}, u32[]{:S(2)}, u32[]{:S(2)}) collective-permute-start(bf16[16,2560]{1,0:T(8,128)(2,1)S(1)} %get-tuple-element.87), channel_id=1, source_target_pairs={{0,2},{1,3},{2,0},{3,1},{4,6},{5,7},{6,4},{7,5},{8,10},{9,11},{10,... | collective-permute-start | bytes 245768 | tf_op jit(solution)/shard_map/ppermute | solution.py:41
  14.3 6.5 %collective-permute-start.4 = (bf16[32,2432]{1,0:T(8,128)(2,1)S(1)}, bf16[32,2432]{1,0:T(8,128)(2,1)S(1)}, u32[]{:S(2)}, u32[]{:S(2)}) collective-permute-start(bf16[32,2432]{1,0:T(8,128)(2,1)S(1)} %get-tuple-element.86), channel_id=1, source_target_pairs={{0,32},{1,33},{2,34},{3,35},{4,36},{5,37},{6,38},{7,39},{8,40},{9,... | collective-permute-start | bytes 466952 | tf_op jit(solution)/shard_map/ppermute | solution.py:41
  15.3 6.5 %collective-permute-start.2 = (bf16[32,2560]{1,0:T(8,128)(2,1)S(1)}, bf16[32,2560]{1,0:T(8,128)(2,1)S(1)}, u32[]{:S(2)}, u32[]{:S(2)}) collective-permute-start(bf16[32,2560]{1,0:T(8,128)(2,1)S(1)} %get-tuple-element.84), channel_id=1, source_target_pairs={{0,4},{1,5},{2,6},{3,7},{4,8},{5,9},{6,10},{7,11},{8,12},{9,13},{1... | collective-permute-start | bytes 491528 | tf_op jit(solution)/shard_map/ppermute | solution.py:41
  15.9 6.5 %collective-permute-start.3 = (bf16[32,2560]{1,0:T(8,128)(2,1)S(1)}, bf16[32,2560]{1,0:T(8,128)(2,1)S(1)}, u32[]{:S(2)}, u32[]{:S(2)}) collective-permute-start(bf16[32,2560]{1,0:T(8,128)(2,1)S(1)} %get-tuple-element.85), channel_id=1, source_target_pairs={{0,1},{1,2},{2,3},{3,0},{4,5},{5,6},{6,7},{7,4},{8,9},{9,10},{10,1... | collective-permute-start | bytes 491528 | tf_op jit(solution)/shard_map/ppermute | solution.py:41
  22.5 8.5 %collective-permute-start.13 = (bf16[64,2432]{1,0:T(8,128)(2,1)S(1)}, bf16[64,2432]{1,0:T(8,128)(2,1)S(1)}, u32[]{:S(2)}, u32[]{:S(2)}) collective-permute-start(bf16[64,2432]{1,0:T(8,128)(2,1)S(1)} %constant_dynamic-update-slice_fusion.6), channel_id=1, source_target_pairs={{0,8},{1,9},{2,10},{3,11},{4,12},{5,13},{6,14},{7,15},{8,0},{9,1},... | collective-permute-start | bytes 933896 | tf_op jit(solution)/shard_map/ppermute | solution.py:41
  24.6 1.7 collective-permute-start.10
  24.6 11.7 %collective-permute-start.12 = (bf16[64,2560]{1,0:T(8,128)(2,1)S(1)}, bf16[64,2560]{1,0:T(8,128)(2,1)S(1)}, u32[]{:S(2)}, u32[]{:S(2)}) collective-permute-start(bf16[64,2560]{1,0:T(8,128)(2,1)S(1)} %constant_dynamic-update-slice_fusion.3), channel_id=1, source_target_pairs={{0,64},{1,65},{2,66},{3,67},{4,68},{5,69},{6,70},{7,71},{8,72},{9,... | collective-permute-start | bytes 983048 | tf_op jit(solution)/shard_map/ppermute | solution.py:41
  25.9 1.6 collective-permute-start.9
  26.1 11.5 %collective-permute-start.11 = (bf16[64,2560]{1,0:T(8,128)(2,1)S(1)}, bf16[64,2560]{1,0:T(8,128)(2,1)S(1)}, u32[]{:S(2)}, u32[]{:S(2)}) collective-permute-start(bf16[64,2560]{1,0:T(8,128)(2,1)S(1)} %constant_dynamic-update-slice_fusion), channel_id=1, source_target_pairs={{0,2},{1,3},{2,0},{3,1},{4,6},{5,7},{6,4},{7,5},{8,10},{9,11},{10,... | collective-permute-start | bytes 983048 | tf_op jit(solution)/shard_map/ppermute | solution.py:41
  26.3 1.7 collective-permute-start.8
  37.6 13.5 %collective-permute-start.14 = (bf16[128,2560]{1,0:T(8,128)(2,1)S(1)}, bf16[128,2560]{1,0:T(8,128)(2,1)S(1)}, u32[]{:S(2)}, u32[]{:S(2)}) collective-permute-start(bf16[128,2560]{1,0:T(8,128)(2,1)S(1)} %pad_maximum_fusion.3.refs_0_), channel_id=1, source_target_pairs={{0,1},{1,2},{2,3},{3,0},{4,5},{5,6},{6,7},{7,4},{8,9},{9,10},{10,1... | collective-permute-start | bytes 1966088 | tf_op jit(solution)/shard_map/ppermute | solution.py:41
  37.6 13.5 %collective-permute-start.15 = (bf16[128,2560]{1,0:T(8,128)(2,1)S(1)}, bf16[128,2560]{1,0:T(8,128)(2,1)S(1)}, u32[]{:S(2)}, u32[]{:S(2)}) collective-permute-start(bf16[128,2560]{1,0:T(8,128)(2,1)S(1)} %pad_maximum_fusion.4.refs_0_), channel_id=1, source_target_pairs={{0,32},{1,33},{2,34},{3,35},{4,36},{5,37},{6,38},{7,39},{8,40},{9,... | collective-permute-start | bytes 1966088 | tf_op jit(solution)/shard_map/ppermute | solution.py:41
  39.5 2.2 %collective-permute-start.19 = (bf16[64,2432]{1,0:T(8,128)(2,1)S(1)}, bf16[64,2432]{1,0:T(8,128)(2,1)S(1)}, u32[]{:S(2)}, u32[]{:S(2)}) collective-permute-start(bf16[64,2432]{1,0:T(8,128)(2,1)S(1)} %collective-permute-done.13.refs_2_), channel_id=1, source_target_pairs={{0,16},{1,17},{2,18},{3,19},{4,20},{5,21},{6,22},{7,23},{8,24},{9,... | collective-permute-start | bytes 933896 | tf_op jit(solution)/shard_map/ppermute | solution.py:41
  39.5 11.6 %collective-permute-start.16 = (bf16[128,2432]{1,0:T(8,128)(2,1)S(1)}, bf16[128,2432]{1,0:T(8,128)(2,1)}, u32[]{:S(2)}, u32[]{:S(2)}) collective-permute-start(bf16[128,2432]{1,0:T(8,128)(2,1)S(1)} %pad_maximum_fusion.5.refs_0_), channel_id=1, source_target_pairs={{0,4},{1,5},{2,6},{3,7},{4,8},{5,9},{6,10},{7,11},{8,12},{9,13},{1... | collective-permute-start | bytes 1867784 | tf_op jit(solution)/shard_map/ppermute | solution.py:41
  41.0 2.7 %collective-permute-start.17 = (bf16[64,2560]{1,0:T(8,128)(2,1)S(1)}, bf16[64,2560]{1,0:T(8,128)(2,1)S(1)}, u32[]{:S(2)}, u32[]{:S(2)}) collective-permute-start(bf16[64,2560]{1,0:T(8,128)(2,1)S(1)} %collective-permute-done.11.refs_2_), channel_id=1, source_target_pairs={{0,16},{1,17},{2,18},{3,19},{4,20},{5,21},{6,22},{7,23},{8,24},{9,... | collective-permute-start | bytes 983048 | tf_op jit(solution)/shard_map/ppermute | solution.py:41
  42.5 2.0 collective-permute-start.18
  51.1 2.4 %collective-permute-start.28 = (bf16[128,2432]{1,0:T(8,128)(2,1)}, bf16[128,2432]{1,0:T(8,128)(2,1)}, u32[]{:S(2)}, u32[]{:S(2)}) collective-permute-start(bf16[128,2432]{1,0:T(8,128)(2,1)} %collective-permute-done.16.refs_1_), channel_id=1, source_target_pairs={{0,16},{1,17},{2,18},{3,19},{4,20},{5,21},{6,22},{7,23},{8,24},{9,... | collective-permute-start | bytes 1867784 | tf_op jit(solution)/shard_map/ppermute | solution.py:41
  51.6 8.6 %collective-permute-start.20 = (bf16[128,2560]{1,0:T(8,128)(2,1)S(1)}, bf16[128,2560]{1,0:T(8,128)(2,1)S(1)}, u32[]{:S(2)}, u32[]{:S(2)}) collective-permute-start(bf16[128,2560]{1,0:T(8,128)(2,1)S(1)} %collective-permute-done.14.refs_1_), channel_id=1, source_target_pairs={{0,16},{1,17},{2,18},{3,19},{4,20},{5,21},{6,22},{7,23},{8,24},{9,... | collective-permute-start | bytes 1966088 | tf_op jit(solution)/shard_map/ppermute | solution.py:41
  51.7 6.0 %collective-permute-start.24 = (bf16[128,2560]{1,0:T(8,128)(2,1)S(1)}, bf16[128,2560]{1,0:T(8,128)(2,1)S(1)}, u32[]{:S(2)}, u32[]{:S(2)}) collective-permute-start(bf16[128,2560]{1,0:T(8,128)(2,1)S(1)} %collective-permute-done.15.refs_1_), channel_id=1, source_target_pairs={{0,16},{1,17},{2,18},{3,19},{4,20},{5,21},{6,22},{7,23},{8,24},{9,... | collective-permute-start | bytes 1966088 | tf_op jit(solution)/shard_map/ppermute | solution.py:41
  52.2 5.5 %copy-start.3 = (bf16[64,2560]{1,0:T(8,128)(2,1)S(1)}, bf16[64,2560]{1,0:T(8,128)(2,1)}, u32[]{:S(2)}) copy-start(bf16[64,2560]{1,0:T(8,128)(2,1)} %copy-done.2) | copy-start | bytes 983044
  52.2 5.5 %copy-start.7 = (bf16[64,2560]{1,0:T(8,128)(2,1)S(1)}, bf16[64,2560]{1,0:T(8,128)(2,1)}, u32[]{:S(2)}) copy-start(bf16[64,2560]{1,0:T(8,128)(2,1)} %copy-done.6) | copy-start | bytes 983044
  57.0 3.2 %copy-start.1 = (bf16[64,2560]{1,0:T(8,128)(2,1)S(1)}, bf16[64,2560]{1,0:T(8,128)(2,1)}, u32[]{:S(2)}) copy-start(bf16[64,2560]{1,0:T(8,128)(2,1)} %copy-done) | copy-start | bytes 983044
  57.0 17.5 %collective-permute-start.29 = (bf16[256,2304]{1,0:T(8,128)(2,1)S(1)}, bf16[256,2304]{1,0:T(8,128)(2,1)S(1)}, u32[]{:S(2)}, u32[]{:S(2)}) collective-permute-start(bf16[256,2304]{1,0:T(8,128)(2,1)S(1)} %get-tuple-element.120), channel_id=1, source_target_pairs={{0,1},{1,2},{2,3},{3,0},{4,5},{5,6},{6,7},{7,4},{8,9},{9,10},{10,1... | collective-permute-start | bytes 3538952 | tf_op jit(solution)/shard_map/ppermute | solution.py:41
  59.6 18.4 %collective-permute-start.25 = (bf16[256,2432]{1,0:T(8,128)(2,1)S(1)}, bf16[256,2432]{1,0:T(8,128)(2,1)S(1)}, u32[]{:S(2)}, u32[]{:S(2)}) collective-permute-start(bf16[256,2432]{1,0:T(8,128)(2,1)S(1)} %get-tuple-element.113), channel_id=1, source_target_pairs={{0,4},{1,5},{2,6},{3,7},{4,8},{5,9},{6,10},{7,11},{8,12},{9,13},{1... | collective-permute-start | bytes 3735560 | tf_op jit(solution)/shard_map/ppermute | solution.py:41
  62.1 18.2 %collective-permute-start.21 = (bf16[256,2432]{1,0:T(8,128)(2,1)S(1)}, bf16[256,2432]{1,0:T(8,128)(2,1)S(1)}, u32[]{:S(2)}, u32[]{:S(2)}) collective-permute-start(bf16[256,2432]{1,0:T(8,128)(2,1)S(1)} %get-tuple-element.106), channel_id=1, source_target_pairs={{0,32},{1,33},{2,34},{3,35},{4,36},{5,37},{6,38},{7,39},{8,40},{9,... | collective-permute-start | bytes 3735560 | tf_op jit(solution)/shard_map/ppermute | solution.py:41
  74.6 7.2 %collective-permute-start.30 = (bf16[128,2304]{1,0:T(8,128)(2,1)S(1)}, bf16[128,2304]{1,0:T(8,128)(2,1)S(1)}, u32[]{:S(2)}, u32[]{:S(2)}) collective-permute-start(bf16[128,2304]{1,0:T(8,128)(2,1)S(1)} %slice.20), channel_id=1, source_target_pairs={{0,16},{1,17},{2,18},{3,19},{4,20},{5,21},{6,22},{7,23},{8,24},{9,... | collective-permute-start | bytes 1769480 | tf_op jit(solution)/shard_map/ppermute | solution.py:41
  78.0 20.5 %collective-permute-start.26 = (bf16[128,2432]{1,0:T(8,128)(2,1)S(1)}, bf16[128,2432]{1,0:T(8,128)(2,1)S(1)}, u32[]{:S(2)}, u32[]{:S(2)}) collective-permute-start(bf16[128,2432]{1,0:T(8,128)(2,1)S(1)} %slice.19), channel_id=1, source_target_pairs={{0,16},{1,17},{2,18},{3,19},{4,20},{5,21},{6,22},{7,23},{8,24},{9,... | collective-permute-start | bytes 1867784 | tf_op jit(solution)/shard_map/ppermute | solution.py:41
  78.5 20.0 %collective-permute-start.27 = (bf16[128,2432]{1,0:T(8,128)(2,1)S(1)}, bf16[128,2432]{1,0:T(8,128)(2,1)S(1)}, u32[]{:S(2)}, u32[]{:S(2)}) collective-permute-start(bf16[128,2432]{1,0:T(8,128)(2,1)S(1)} %get-tuple-element.115), channel_id=1, source_target_pairs={{0,8},{1,9},{2,10},{3,11},{4,12},{5,13},{6,14},{7,15},{8,0},{9,1},... | collective-permute-start | bytes 1867784 | tf_op jit(solution)/shard_map/ppermute | solution.py:41
  80.3 18.3 %copy-start.12 = (bf16[256,2432]{1,0:T(8,128)(2,1)}, bf16[256,2432]{1,0:T(8,128)(2,1)S(1)}, u32[]{:S(2)}) copy-start(bf16[256,2432]{1,0:T(8,128)(2,1)S(1)} %collective-permute-done.21.refs_1_) | copy-start | bytes 3735556
  80.3 18.2 %collective-permute-start.22 = (bf16[128,2432]{1,0:T(8,128)(2,1)S(1)}, bf16[128,2432]{1,0:T(8,128)(2,1)S(1)}, u32[]{:S(2)}, u32[]{:S(2)}) collective-permute-start(bf16[128,2432]{1,0:T(8,128)(2,1)S(1)} %slice.18), channel_id=1, source_target_pairs={{0,16},{1,17},{2,18},{3,19},{4,20},{5,21},{6,22},{7,23},{8,24},{9,... | collective-permute-start | bytes 1867784 | tf_op jit(solution)/shard_map/ppermute | solution.py:41
  80.5 18.0 %collective-permute-start.23 = (bf16[128,2432]{1,0:T(8,128)(2,1)S(1)}, bf16[128,2432]{1,0:T(8,128)(2,1)S(1)}, u32[]{:S(2)}, u32[]{:S(2)}) collective-permute-start(bf16[128,2432]{1,0:T(8,128)(2,1)S(1)} %get-tuple-element.108), channel_id=1, source_target_pairs={{0,64},{1,65},{2,66},{3,67},{4,68},{5,69},{6,70},{7,71},{8,72},{9,... | collective-permute-start | bytes 1867784 | tf_op jit(solution)/shard_map/ppermute | solution.py:41
  81.7 16.8 %collective-permute-start.31 = (bf16[128,2304]{1,0:T(8,128)(2,1)S(1)}, bf16[128,2304]{1,0:T(8,128)(2,1)S(1)}, u32[]{:S(2)}, u32[]{:S(2)}) collective-permute-start(bf16[128,2304]{1,0:T(8,128)(2,1)S(1)} %get-tuple-element.122), channel_id=1, source_target_pairs={{0,2},{1,3},{2,0},{3,1},{4,6},{5,7},{6,4},{7,5},{8,10},{9,11},{10,... | collective-permute-start | bytes 1769480 | tf_op jit(solution)/shard_map/ppermute | solution.py:41
  118.8 3.6 %collective-permute-start.40 = (bf16[128,2432]{1,0:T(8,128)(2,1)S(1)}, bf16[128,2432]{1,0:T(8,128)(2,1)S(1)}, u32[]{:S(2)}, u32[]{:S(2)}) collective-permute-start(bf16[128,2432]{1,0:T(8,128)(2,1)S(1)} %get-tuple-element.136), channel_id=1, source_target_pairs={{0,16},{1,17},{2,18},{3,19},{4,20},{5,21},{6,22},{7,23},{8,24},{9,... | collective-permute-start | bytes 1867784 | tf_op jit(solution)/shard_map/ppermute | solution.py:41
  119.2 5.2 %collective-permute-start.32 = (bf16[128,2432]{1,0:T(8,128)(2,1)S(1)}, bf16[128,2432]{1,0:T(8,128)(2,1)S(1)}, u32[]{:S(2)}, u32[]{:S(2)}) collective-permute-start(bf16[128,2432]{1,0:T(8,128)(2,1)S(1)} %get-tuple-element.125), channel_id=1, source_target_pairs={{0,16},{1,17},{2,18},{3,19},{4,20},{5,21},{6,22},{7,23},{8,24},{9,... | collective-permute-start | bytes 1867784 | tf_op jit(solution)/shard_map/ppermute | solution.py:41
  119.7 6.5 %collective-permute-start.48 = (bf16[128,2304]{1,0:T(8,128)(2,1)S(1)}, bf16[128,2304]{1,0:T(8,128)(2,1)S(1)}, u32[]{:S(2)}, u32[]{:S(2)}) collective-permute-start(bf16[128,2304]{1,0:T(8,128)(2,1)S(1)} %get-tuple-element.147), channel_id=1, source_target_pairs={{0,16},{1,17},{2,18},{3,19},{4,20},{5,21},{6,22},{7,23},{8,24},{9,... | collective-permute-start | bytes 1769480 | tf_op jit(solution)/shard_map/ppermute | solution.py:41
  119.7 18.4 %collective-permute-start.42 = (bf16[128,2432]{1,0:T(8,128)(2,1)S(1)}, bf16[128,2432]{1,0:T(8,128)(2,1)S(1)}, u32[]{:S(2)}, u32[]{:S(2)}) collective-permute-start(bf16[128,2432]{1,0:T(8,128)(2,1)S(1)} %get-tuple-element.137), channel_id=1, source_target_pairs={{0,8},{1,9},{2,10},{3,11},{4,12},{5,13},{6,14},{7,15},{8,0},{9,1},... | collective-permute-start | bytes 1867784 | tf_op jit(solution)/shard_map/ppermute | solution.py:41
  122.5 28.8 %collective-permute-start.41 = (bf16[256,2432]{1,0:T(8,128)(2,1)S(1)}, bf16[256,2432]{1,0:T(8,128)(2,1)S(1)}, u32[]{:S(2)}, u32[]{:S(2)}) collective-permute-start(bf16[256,2432]{1,0:T(8,128)(2,1)S(1)} %pad_maximum_fusion.1), channel_id=1, source_target_pairs={{0,12},{1,13},{2,14},{3,15},{4,0},{5,1},{6,2},{7,3},{8,4},{9,5},{1... | collective-permute-start | bytes 3735560 | tf_op jit(solution)/shard_map/ppermute | solution.py:41
  124.4 27.5 %collective-permute-start.33 = (bf16[256,2432]{1,0:T(8,128)(2,1)S(1)}, bf16[256,2432]{1,0:T(8,128)(2,1)S(1)}, u32[]{:S(2)}, u32[]{:S(2)}) collective-permute-start(bf16[256,2432]{1,0:T(8,128)(2,1)S(1)} %pad_maximum_fusion), channel_id=1, source_target_pairs={{0,96},{1,97},{2,98},{3,99},{4,100},{5,101},{6,102},{7,103},{8,104... | collective-permute-start | bytes 3735560 | tf_op jit(solution)/shard_map/ppermute | solution.py:41
  126.3 28.9 %collective-permute-start.49 = (bf16[256,2304]{1,0:T(8,128)(2,1)S(1)}, bf16[256,2304]{1,0:T(8,128)(2,1)S(1)}, u32[]{:S(2)}, u32[]{:S(2)}) collective-permute-start(bf16[256,2304]{1,0:T(8,128)(2,1)S(1)} %pad_maximum_fusion.2), channel_id=1, source_target_pairs={{0,3},{1,0},{2,1},{3,2},{4,7},{5,4},{6,5},{7,6},{8,11},{9,8},{10,9... | collective-permute-start | bytes 3538952 | tf_op jit(solution)/shard_map/ppermute | solution.py:41
  128.0 23.9 %collective-permute-start.34 = (bf16[128,2432]{1,0:T(8,128)(2,1)S(1)}, bf16[128,2432]{1,0:T(8,128)(2,1)S(1)}, u32[]{:S(2)}, u32[]{:S(2)}) collective-permute-start(bf16[128,2432]{1,0:T(8,128)(2,1)S(1)} %get-tuple-element.126), channel_id=1, source_target_pairs={{0,64},{1,65},{2,66},{3,67},{4,68},{5,69},{6,70},{7,71},{8,72},{9,... | collective-permute-start | bytes 1867784 | tf_op jit(solution)/shard_map/ppermute | solution.py:41
  138.1 17.1 %collective-permute-start.50 = (bf16[128,2304]{1,0:T(8,128)(2,1)S(1)}, bf16[128,2304]{1,0:T(8,128)(2,1)S(1)}, u32[]{:S(2)}, u32[]{:S(2)}) collective-permute-start(bf16[128,2304]{1,0:T(8,128)(2,1)S(1)} %get-tuple-element.148), channel_id=1, source_target_pairs={{0,2},{1,3},{2,0},{3,1},{4,6},{5,7},{6,4},{7,5},{8,10},{9,11},{10,... | collective-permute-start | bytes 1769480 | tf_op jit(solution)/shard_map/ppermute | solution.py:41
  151.8 4.0 %collective-permute-start.43 = (bf16[256,2432]{1,0:T(8,128)(2,1)S(1)}, bf16[256,2432]{1,0:T(8,128)(2,1)S(1)}, u32[]{:S(2)}, u32[]{:S(2)}) collective-permute-start(bf16[256,2432]{1,0:T(8,128)(2,1)S(1)} %other1.1), channel_id=1, source_target_pairs={{0,16},{1,17},{2,18},{3,19},{4,20},{5,21},{6,22},{7,23},{8,24},{9,... | collective-permute-start | bytes 3735560 | tf_op jit(solution)/shard_map/ppermute | solution.py:41
  152.4 7.5 %collective-permute-start.35 = (bf16[256,2432]{1,0:T(8,128)(2,1)S(1)}, bf16[256,2432]{1,0:T(8,128)(2,1)S(1)}, u32[]{:S(2)}, u32[]{:S(2)}) collective-permute-start(bf16[256,2432]{1,0:T(8,128)(2,1)S(1)} %other0.1), channel_id=1, source_target_pairs={{0,16},{1,17},{2,18},{3,19},{4,20},{5,21},{6,22},{7,23},{8,24},{9,... | collective-permute-start | bytes 3735560 | tf_op jit(solution)/shard_map/ppermute | solution.py:41
  155.7 6.9 %collective-permute-start.51 = (bf16[256,2304]{1,0:T(8,128)(2,1)S(1)}, bf16[256,2304]{1,0:T(8,128)(2,1)S(1)}, u32[]{:S(2)}, u32[]{:S(2)}) collective-permute-start(bf16[256,2304]{1,0:T(8,128)(2,1)S(1)} %other2.1), channel_id=1, source_target_pairs={{0,16},{1,17},{2,18},{3,19},{4,20},{5,21},{6,22},{7,23},{8,24},{9,... | collective-permute-start | bytes 3538952 | tf_op jit(solution)/shard_map/ppermute | solution.py:41
  156.3 11.5 %collective-permute-start.44 = (bf16[128,2432]{1,0:T(8,128)(2,1)S(1)}, bf16[128,2432]{1,0:T(8,128)(2,1)S(1)}, u32[]{:S(2)}, u32[]{:S(2)}) collective-permute-start(bf16[128,2432]{1,0:T(8,128)(2,1)S(1)} %get-tuple-element.140), channel_id=1, source_target_pairs={{0,96},{1,97},{2,98},{3,99},{4,100},{5,101},{6,102},{7,103},{8,104... | collective-permute-start | bytes 1867784 | tf_op jit(solution)/shard_map/ppermute | solution.py:41
  160.4 10.3 %collective-permute-start.36 = (bf16[128,2432]{1,0:T(8,128)(2,1)S(1)}, bf16[128,2432]{1,0:T(8,128)(2,1)S(1)}, u32[]{:S(2)}, u32[]{:S(2)}) collective-permute-start(bf16[128,2432]{1,0:T(8,128)(2,1)S(1)} %get-tuple-element.129), channel_id=1, source_target_pairs={{0,3},{1,0},{2,1},{3,2},{4,7},{5,4},{6,5},{7,6},{8,11},{9,8},{10,9... | collective-permute-start | bytes 1867784 | tf_op jit(solution)/shard_map/ppermute | solution.py:41
  163.1 11.4 %collective-permute-start.52 = (bf16[128,2304]{1,0:T(8,128)(2,1)S(1)}, bf16[128,2304]{1,0:T(8,128)(2,1)S(1)}, u32[]{:S(2)}, u32[]{:S(2)}) collective-permute-start(bf16[128,2304]{1,0:T(8,128)(2,1)S(1)} %get-tuple-element.151), channel_id=1, source_target_pairs={{0,12},{1,13},{2,14},{3,15},{4,0},{5,1},{6,2},{7,3},{8,4},{9,5},{1... | collective-permute-start | bytes 1769480 | tf_op jit(solution)/shard_map/ppermute | solution.py:41
  167.8 6.9 %collective-permute-start.46 = (bf16[64,2432]{1,0:T(8,128)(2,1)S(1)}, bf16[64,2432]{1,0:T(8,128)(2,1)S(1)}, u32[]{:S(2)}, u32[]{:S(2)}) collective-permute-start(bf16[64,2432]{1,0:T(8,128)(2,1)S(1)} %slice.22), channel_id=1, source_target_pairs={{0,16},{1,17},{2,18},{3,19},{4,20},{5,21},{6,22},{7,23},{8,24},{9,... | collective-permute-start | bytes 933896 | tf_op jit(solution)/shard_map/ppermute | solution.py:41
  167.9 11.3 %collective-permute-start.45 = (bf16[64,2432]{1,0:T(8,128)(2,1)S(1)}, bf16[64,2432]{1,0:T(8,128)(2,1)S(1)}, u32[]{:S(2)}, u32[]{:S(2)}) collective-permute-start(bf16[64,2432]{1,0:T(8,128)(2,1)S(1)} %get-tuple-element.142), channel_id=1, source_target_pairs={{0,64},{1,65},{2,66},{3,67},{4,68},{5,69},{6,70},{7,71},{8,72},{9,... | collective-permute-start | bytes 933896 | tf_op jit(solution)/shard_map/ppermute | solution.py:41
  170.7 10.7 %collective-permute-start.38 = (bf16[64,2432]{1,0:T(8,128)(2,1)S(1)}, bf16[64,2432]{1,0:T(8,128)(2,1)S(1)}, u32[]{:S(2)}, u32[]{:S(2)}) collective-permute-start(bf16[64,2432]{1,0:T(8,128)(2,1)S(1)} %slice.21), channel_id=1, source_target_pairs={{0,16},{1,17},{2,18},{3,19},{4,20},{5,21},{6,22},{7,23},{8,24},{9,... | collective-permute-start | bytes 933896 | tf_op jit(solution)/shard_map/ppermute | solution.py:41
  170.8 11.6 %collective-permute-start.37 = (bf16[64,2432]{1,0:T(8,128)(2,1)S(1)}, bf16[64,2432]{1,0:T(8,128)(2,1)S(1)}, u32[]{:S(2)}, u32[]{:S(2)}) collective-permute-start(bf16[64,2432]{1,0:T(8,128)(2,1)S(1)} %get-tuple-element.131), channel_id=1, source_target_pairs={{0,2},{1,3},{2,0},{3,1},{4,6},{5,7},{6,4},{7,5},{8,10},{9,11},{10,... | collective-permute-start | bytes 933896 | tf_op jit(solution)/shard_map/ppermute | solution.py:41
  174.5 8.9 %collective-permute-start.54 = (bf16[64,2304]{1,0:T(8,128)(2,1)S(1)}, bf16[64,2304]{1,0:T(8,128)(2,1)S(1)}, u32[]{:S(2)}, u32[]{:S(2)}) collective-permute-start(bf16[64,2304]{1,0:T(8,128)(2,1)S(1)} %slice.23), channel_id=1, source_target_pairs={{0,16},{1,17},{2,18},{3,19},{4,20},{5,21},{6,22},{7,23},{8,24},{9,... | collective-permute-start | bytes 884744 | tf_op jit(solution)/shard_map/ppermute | solution.py:41
  174.7 11.3 %collective-permute-start.53 = (bf16[64,2304]{1,0:T(8,128)(2,1)S(1)}, bf16[64,2304]{1,0:T(8,128)(2,1)S(1)}, u32[]{:S(2)}, u32[]{:S(2)}) collective-permute-start(bf16[64,2304]{1,0:T(8,128)(2,1)S(1)} %get-tuple-element.153), channel_id=1, source_target_pairs={{0,8},{1,9},{2,10},{3,11},{4,12},{5,13},{6,14},{7,15},{8,0},{9,1},... | collective-permute-start | bytes 884744 | tf_op jit(solution)/shard_map/ppermute | solution.py:41
  179.3 12.1 %collective-permute-start.47 = (bf16[32,2432]{1,0:T(8,128)(2,1)S(1)}, bf16[32,2432]{1,0:T(8,128)(2,1)S(1)}, u32[]{:S(2)}, u32[]{:S(2)}) collective-permute-start(bf16[32,2432]{1,0:T(8,128)(2,1)S(1)} %get-tuple-element.143), channel_id=1, source_target_pairs={{0,3},{1,0},{2,1},{3,2},{4,7},{5,4},{6,5},{7,6},{8,11},{9,8},{10,9... | collective-permute-start | bytes 466952 | tf_op jit(solution)/shard_map/ppermute | solution.py:41
  182.6 8.8 %collective-permute-start.39 = (bf16[32,2432]{1,0:T(8,128)(2,1)S(1)}, bf16[32,2432]{1,0:T(8,128)(2,1)S(1)}, u32[]{:S(2)}, u32[]{:S(2)}) collective-permute-start(bf16[32,2432]{1,0:T(8,128)(2,1)S(1)} %get-tuple-element.132), channel_id=1, source_target_pairs={{0,12},{1,13},{2,14},{3,15},{4,0},{5,1},{6,2},{7,3},{8,4},{9,5},{1... | collective-permute-start | bytes 466952 | tf_op jit(solution)/shard_map/ppermute | solution.py:41
  186.1 5.2 %collective-permute-start.55 = (bf16[32,2304]{1,0:T(8,128)(2,1)S(1)}, bf16[32,2304]{1,0:T(8,128)(2,1)S(1)}, u32[]{:S(2)}, u32[]{:S(2)}) collective-permute-start(bf16[32,2304]{1,0:T(8,128)(2,1)S(1)} %get-tuple-element.154), channel_id=1, source_target_pairs={{0,96},{1,97},{2,98},{3,99},{4,100},{5,101},{6,102},{7,103},{8,104... | collective-permute-start | bytes 442376 | tf_op jit(solution)/shard_map/ppermute | solution.py:41
  191.4 8.3 %collective-permute-start.56 = (bf16[16,7168]{1,0:T(8,128)(2,1)S(1)}, bf16[16,7168]{1,0:T(8,128)(2,1)S(1)}, u32[]{:S(2)}, u32[]{:S(2)}) collective-permute-start(bf16[16,7168]{1,0:T(8,128)(2,1)S(1)} %cross.1), channel_id=1, source_target_pairs={{0,16},{1,17},{2,18},{3,19},{4,20},{5,21},{6,22},{7,23},{8,24},{9,... | collective-permute-start | bytes 688136 | tf_op jit(solution)/shard_map/ppermute | solution.py:41
  191.5 8.2 %collective-permute-start.58 = (bf16[16,2432]{1,0:T(8,128)(2,1)S(1)}, bf16[16,2432]{1,0:T(8,128)(2,1)S(1)}, u32[]{:S(2)}, u32[]{:S(2)}) collective-permute-start(bf16[16,2432]{1,0:T(8,128)(2,1)S(1)} %get-tuple-element.158), channel_id=1, source_target_pairs={{0,2},{1,3},{2,0},{3,1},{4,6},{5,7},{6,4},{7,5},{8,10},{9,11},{10,... | collective-permute-start | bytes 233480 | tf_op jit(solution)/shard_map/ppermute | solution.py:41
  192.7 6.9 %collective-permute-start.57 = (bf16[16,2432]{1,0:T(8,128)(2,1)S(1)}, bf16[16,2432]{1,0:T(8,128)(2,1)S(1)}, u32[]{:S(2)}, u32[]{:S(2)}) collective-permute-start(bf16[16,2432]{1,0:T(8,128)(2,1)S(1)} %get-tuple-element.156), channel_id=1, source_target_pairs={{0,8},{1,9},{2,10},{3,11},{4,12},{5,13},{6,14},{7,15},{8,0},{9,1},... | collective-permute-start | bytes 233480 | tf_op jit(solution)/shard_map/ppermute | solution.py:41
  193.8 5.9 %collective-permute-start.59 = (bf16[16,2304]{1,0:T(8,128)(2,1)S(1)}, bf16[16,2304]{1,0:T(8,128)(2,1)S(1)}, u32[]{:S(2)}, u32[]{:S(2)}) collective-permute-start(bf16[16,2304]{1,0:T(8,128)(2,1)S(1)} %get-tuple-element.160), channel_id=1, source_target_pairs={{0,64},{1,65},{2,66},{3,67},{4,68},{5,69},{6,70},{7,71},{8,72},{9,... | collective-permute-start | bytes 221192 | tf_op jit(solution)/shard_map/ppermute | solution.py:41
  (9 other events, 11.0 us)
